TPU v7x, 32 devices: a whole 2x2x4 slice. The times are simulated.
32 devices in a mesh: dp: 32 (over z, y, x, core).
Axes of the slice: x: 2, y: 2, z: 4, core: 2. Of those that a mesh axis runs over, the one named last changes fastest.
Arguments:
- token_ids: int32 [256, 512], P('dp'), may hold values from 0 to 30521
- lengths: int32 [256], P('dp'), may hold values from 85 to 512, as said below
- gate_noise: float32 [1284], replicated, may hold values from 0.02 to 0.98
- lagrange: float32 [2], replicated, may hold values from 1 to 3
- teacher_table: bfloat16 [31034, 256], replicated, may hold values from -0.29882812 to 0.29882812
- teacher_flat: bfloat16 [790016], replicated, may hold values from -5 to 7
- word_table: float32 [31232, 256], P('dp'), may hold values from -0.3 to 0.3
- table_first: float32 [31232, 256], P('dp'), may hold values from -3.5762787e-07 to 3.5762787e-07
- table_second: float32 [31232, 256], P('dp'), may hold values from 2.917711e-16 to 1.1670845e-15
- layer_flat: float32 [860160], P('dp'), may hold values from -5 to 7
- flat_first: float32 [860160], P('dp'), may hold values from -1.4305115e-06 to 1.4305115e-06
- flat_second: float32 [860160], P('dp'), may hold values from 4.668338e-15 to 1.8673351e-14
Outputs:
- table_out: float32 [31232, 256], P('dp')
- table_first_out: float32 [31232, 256], P('dp')
- table_second_out: float32 [31232, 256], P('dp')
- flat_out: float32 [860160], P('dp')
- flat_first_out: float32 [860160], P('dp')
- flat_second_out: float32 [860160], P('dp')
- total_loss: float32 [], replicated
- grad_norm: float32 [], replicated
Inputs may be any that keep to these rules, and one draw needn't show every extreme that they name: `lengths`: the first of each device's 8 sequences is its longest; the longest on device d (from 0) is 170 + 342 * d // (devices - 1), the others are at least half of it.
All inputs are finite; a program needn't handle non-finite values.
Results may differ from a plain program's by a relative error of at most 0.0061.
Values may be sent and summed in bfloat16 or wider, within the bound.
A program may use at most 256 MiB of HBM per device.

v0:
```python
import math

import jax
import jax.numpy as jnp
from jax import lax
from jax.sharding import PartitionSpec as P

D = 256
HEADS = 4
FF = 1024
VOCAB = 30522
ADAM_STEP = 10
NPAR = 856836


clip_norm = 0.002
learn_rate = 0.015
beta_one = 0.9
beta_two = 0.999
adam_eps = 1e-08
decay_rate = 0.01
sparse_target = 0.3
relaxation_heat = 2.0 / 3.0
widened_left_limit = -0.1
widened_right_limit = 1.1
norm_eps = 1e-12


def layout(student):
    square = (D, D)
    entries = [("w_query", square), ("w_key", square), ("w_value", square), ("w_output", square)]
    if student:
        entries = entries + [("w_align", square)]
    entries = entries + [
        ("w_up", (D, FF)),
        ("w_down", (FF, D)),
        ("vectors", (10, D)),
        ("b_up", (FF,)),
    ]
    if student:
        entries = entries + [("gate_logits", (D + HEADS + FF,))]
    return entries


def unpack(flat_vector, student):
    pieces = {}
    offset = 0
    for entry_name, entry_shape in layout(student):
        length = math.prod(entry_shape)
        pieces[entry_name] = flat_vector[offset : offset + length].reshape(entry_shape)
        offset = offset + length
    return pieces


def layer_norm(inputs, gain_row, bias_row):
    row_mean = jnp.mean(inputs, axis=-1, keepdims=True)
    centred = inputs - row_mean
    variance = jnp.mean(centred * centred, axis=-1, keepdims=True)
    return centred * lax.rsqrt(variance + norm_eps) * gain_row + bias_row


def exact_gelu(inputs):
    return jax.nn.gelu(inputs, approximate=False)


def gate_values(mask_logodds, flat_random_sample):
    logistic_function = jax.nn.sigmoid(
        (jnp.log(flat_random_sample) - jnp.log(1.0 - flat_random_sample) + mask_logodds)
        / relaxation_heat
    )
    return jnp.clip(
        logistic_function * (widened_right_limit - widened_left_limit) + widened_left_limit,
        0.0,
        1.0,
    )


def lagrangian(mask_logodds, lagrange):
    survival_probability = jax.nn.sigmoid(
        mask_logodds - relaxation_heat * math.log(-widened_left_limit / widened_right_limit)
    )
    head_dim = D // HEADS
    kept_hidden = jnp.mean(survival_probability[:D])
    kept_rest = 4.0 * head_dim * jnp.sum(survival_probability[D : D + HEADS]) + 2.0 * jnp.sum(
        survival_probability[D + HEADS :]
    )
    expected = kept_hidden * kept_rest / (4.0 * D + 2.0 * FF)
    excess = expected - sparse_target
    return lagrange[0] * excess + lagrange[1] * excess * excess


def dense_mm(left, right):
    return jnp.dot(left, right, preferred_element_type=jnp.float32)


def column_sum(grad_low):
    return jnp.sum(grad_low.astype(jnp.float32), axis=0)


def embed_tokens(table_rows, token_ids):
    seq_count, seq_span = token_ids.shape
    picked = jnp.take(table_rows, token_ids.reshape(-1), axis=0).astype(jnp.float32)
    places = table_rows[VOCAB : VOCAB + seq_span].astype(jnp.float32)
    return (picked.reshape(seq_count, seq_span, D) + places[None]).reshape(seq_count * seq_span, D)


def attend(queries, keys_low, values, key_valid):
    factor = queries.shape[-1] ** (-0.5)
    scores = (
        jnp.einsum("qhd,khd->hqk", queries, keys_low, preferred_element_type=jnp.float32) * factor
    )
    scores = jnp.where(key_valid[None, None, :] > 0, scores, -1e30)
    largest = jnp.max(scores, axis=-1, keepdims=True)
    log_total = jnp.log(jnp.sum(jnp.exp(scores - largest), axis=-1, keepdims=True)) + largest
    shares_low = jnp.exp(scores - log_total).astype(jnp.bfloat16)
    context = jnp.einsum("hqk,khd->qhd", shares_low, values, preferred_element_type=jnp.float32)
    return (context, log_total[..., 0])


def attend_back(queries, keys_low, values, key_valid, log_total, d_context):
    factor = queries.shape[-1] ** (-0.5)
    scores = (
        jnp.einsum("qhd,khd->hqk", queries, keys_low, preferred_element_type=jnp.float32) * factor
    )
    scores = jnp.where(key_valid[None, None, :] > 0, scores, -1e30)
    shares = jnp.exp(scores - log_total[..., None])
    d_values = jnp.einsum(
        "hqk,qhd->khd", shares.astype(jnp.bfloat16), d_context, preferred_element_type=jnp.float32
    )
    d_shares = jnp.einsum("qhd,khd->hqk", d_context, values, preferred_element_type=jnp.float32)
    d_scores = (shares * (d_shares - jnp.sum(shares * d_shares, axis=-1, keepdims=True))).astype(
        jnp.bfloat16
    )
    d_queries = (
        jnp.einsum("hqk,khd->qhd", d_scores, keys_low, preferred_element_type=jnp.float32) * factor
    )
    d_keys = (
        jnp.einsum("hqk,qhd->khd", d_scores, queries, preferred_element_type=jnp.float32) * factor
    )
    return (
        d_queries.astype(jnp.bfloat16),
        d_keys.astype(jnp.bfloat16),
        d_values.astype(jnp.bfloat16),
    )


def forward(table_rows, weights, token_ids, lengths, gate_set):
    gate_hidden, gate_heads, gate_inner = gate_set
    seq_count, seq_span = token_ids.shape
    vectors = weights["vectors"].astype(jnp.float32)
    embedded = embed_tokens(table_rows, token_ids)
    start_f = layer_norm(embedded, vectors[0], vectors[1]) * gate_hidden
    start_low = start_f.astype(jnp.bfloat16)
    head_split = (seq_count, seq_span, HEADS, D // HEADS)
    queries = (
        (dense_mm(start_low, weights["w_query"]) + vectors[6])
        .astype(jnp.bfloat16)
        .reshape(head_split)
    )
    keys_low = dense_mm(start_low, weights["w_key"]).astype(jnp.bfloat16).reshape(head_split)
    values = (
        (dense_mm(start_low, weights["w_value"]) + vectors[7])
        .astype(jnp.bfloat16)
        .reshape(head_split)
    )
    key_valid = (jnp.arange(seq_span)[None, :] < lengths[:, None]).astype(jnp.float32)
    context, log_total = lax.map(
        lambda group_in: attend(*group_in), (queries, keys_low, values, key_valid)
    )
    gated_low = (
        (context * gate_heads[:, None]).reshape(seq_count * seq_span, D).astype(jnp.bfloat16)
    )
    branch = dense_mm(gated_low, weights["w_output"]) + vectors[8]
    first_sum = start_f + gate_hidden * branch
    middle = layer_norm(first_sum, vectors[2], vectors[3])
    middle_low = middle.astype(jnp.bfloat16)
    pre_up = dense_mm(middle_low, weights["w_up"]) + weights["b_up"].astype(jnp.float32)
    up_low = (exact_gelu(pre_up) * gate_inner).astype(jnp.bfloat16)
    down_out = dense_mm(up_low, weights["w_down"]) + vectors[9]
    second_sum = middle + gate_hidden * down_out
    output = layer_norm(second_sum, vectors[4], vectors[5])
    saved_acts = {
        "embedded": embedded,
        "start_low": start_low,
        "queries": queries,
        "keys_low": keys_low,
        "values": values,
        "key_valid": key_valid,
        "log_total": log_total,
        "context": context,
        "gated_low": gated_low,
        "branch": branch,
        "first_sum": first_sum,
        "middle_low": middle_low,
        "pre_up": pre_up,
        "up_low": up_low,
        "down_out": down_out,
        "second_sum": second_sum,
    }
    return (output, saved_acts)


def backward(weights, saved_acts, gate_set, d_output):
    gate_hidden, gate_heads, gate_inner = gate_set
    vectors = weights["vectors"].astype(jnp.float32)
    seq_count, seq_span = saved_acts["key_valid"].shape
    token_rows = seq_count * seq_span
    _, pull_back = jax.vjp(layer_norm, saved_acts["second_sum"], vectors[4], vectors[5])
    d_second, d_gain_two, d_bias_two = pull_back(d_output)
    d_down = (d_second * gate_hidden).astype(jnp.bfloat16)
    d_hidden = jnp.sum(d_second * saved_acts["down_out"], axis=0)
    d_w_down = jnp.einsum(
        "ti,td->id", saved_acts["up_low"], d_down, preferred_element_type=jnp.float32
    )
    d_up = jnp.einsum("td,id->ti", d_down, weights["w_down"], preferred_element_type=jnp.float32)
    activated, gelu_back = jax.vjp(exact_gelu, saved_acts["pre_up"])
    d_inner = jnp.sum(d_up * activated, axis=0)
    d_pre = gelu_back(d_up * gate_inner)[0].astype(jnp.bfloat16)
    d_w_up = jnp.einsum(
        "td,ti->di", saved_acts["middle_low"], d_pre, preferred_element_type=jnp.float32
    )
    d_middle = d_second + jnp.einsum(
        "ti,di->td", d_pre, weights["w_up"], preferred_element_type=jnp.float32
    )
    _, pull_back = jax.vjp(layer_norm, saved_acts["first_sum"], vectors[2], vectors[3])
    d_first, d_gain_one, d_bias_one = pull_back(d_middle)
    d_branch = (d_first * gate_hidden).astype(jnp.bfloat16)
    d_hidden = d_hidden + jnp.sum(d_first * saved_acts["branch"], axis=0)
    d_w_output = jnp.einsum(
        "td,te->de", saved_acts["gated_low"], d_branch, preferred_element_type=jnp.float32
    )
    d_gated = jnp.einsum(
        "te,de->td", d_branch, weights["w_output"], preferred_element_type=jnp.float32
    ).reshape(saved_acts["context"].shape)
    d_heads = jnp.sum(d_gated * saved_acts["context"], axis=(0, 1, 3))
    d_context = (d_gated * gate_heads[:, None]).astype(jnp.bfloat16)
    d_queries, d_keys, d_values = lax.map(
        lambda group_in: attend_back(*group_in),
        (
            saved_acts["queries"],
            saved_acts["keys_low"],
            saved_acts["values"],
            saved_acts["key_valid"],
            saved_acts["log_total"],
            d_context,
        ),
    )
    d_queries = d_queries.reshape(token_rows, D)
    d_keys = d_keys.reshape(token_rows, D)
    d_values = d_values.reshape(token_rows, D)
    start_low = saved_acts["start_low"]
    d_w_query = jnp.einsum("td,te->de", start_low, d_queries, preferred_element_type=jnp.float32)
    d_w_key = jnp.einsum("td,te->de", start_low, d_keys, preferred_element_type=jnp.float32)
    d_w_value = jnp.einsum("td,te->de", start_low, d_values, preferred_element_type=jnp.float32)
    d_start = d_first + jnp.einsum(
        "te,de->td", d_queries, weights["w_query"], preferred_element_type=jnp.float32
    )
    d_start = d_start + jnp.einsum(
        "te,de->td", d_keys, weights["w_key"], preferred_element_type=jnp.float32
    )
    d_start = d_start + jnp.einsum(
        "te,de->td", d_values, weights["w_value"], preferred_element_type=jnp.float32
    )
    normed, pull_back = jax.vjp(layer_norm, saved_acts["embedded"], vectors[0], vectors[1])
    d_hidden = d_hidden + jnp.sum(d_start * normed, axis=0)
    d_embedded, d_gain_emb, d_bias_emb = pull_back(d_start * gate_hidden)
    d_vectors = jnp.stack(
        [
            d_gain_emb,
            d_bias_emb,
            d_gain_one,
            d_bias_one,
            d_gain_two,
            d_bias_two,
            column_sum(d_queries),
            column_sum(d_values),
            column_sum(d_branch),
            column_sum(d_down),
        ]
    )
    grad_map = {
        "w_query": d_w_query,
        "w_key": d_w_key,
        "w_value": d_w_value,
        "w_output": d_w_output,
        "w_up": d_w_up,
        "w_down": d_w_down,
        "vectors": d_vectors,
        "b_up": column_sum(d_pre),
    }
    return (grad_map, d_embedded, (d_hidden, d_heads, d_inner))


def table_term(d_embedded, token_ids, total_rows):
    seq_count, seq_span = token_ids.shape
    place_rows = VOCAB + jnp.arange(seq_span, dtype=jnp.int32)
    index_all = jnp.concatenate([token_ids.reshape(-1), place_rows])
    updates = jnp.concatenate(
        [d_embedded, jnp.sum(d_embedded.reshape(seq_count, seq_span, D), axis=0)]
    )
    return jnp.zeros((total_rows, D), jnp.float32).at[index_all].add(updates)


def adam_step(weight, first_old, second, clipped):
    first_new = beta_one * first_old + (1.0 - beta_one) * clipped
    second_new = beta_two * second + (1.0 - beta_two) * clipped * clipped
    first_hat = first_new / (1.0 - beta_one**ADAM_STEP)
    second_hat = second_new / (1.0 - beta_two**ADAM_STEP)
    weight_new = weight - learn_rate * (
        first_hat / (jnp.sqrt(second_hat) + adam_eps) + decay_rate * weight
    )
    return (weight_new, first_new, second_new)


def per_device(
    token_ids,
    lengths,
    gate_noise,
    lagrange,
    teacher_table,
    teacher_flat,
    word_table,
    table_first,
    table_second,
    layer_flat,
    flat_first,
    flat_second,
):
    table_rows, flat_rows = (
        lax.all_gather(word_table.astype(jnp.bfloat16), "dp", axis=0, tiled=True),
        lax.all_gather(layer_flat.astype(jnp.bfloat16), "dp", axis=0, tiled=True),
    )
    global_count = lax.psum(jnp.sum(lengths).astype(jnp.float32), "dp")
    weights = unpack(flat_rows, True)
    mask_logodds = weights["gate_logits"].astype(jnp.float32)
    gate_all, gate_back = jax.vjp(lambda logit_in: gate_values(logit_in, gate_noise), mask_logodds)
    gate_set = (gate_all[:D], gate_all[D : D + HEADS], gate_all[D + HEADS :])
    all_open = (
        jnp.ones((D,), jnp.float32),
        jnp.ones((HEADS,), jnp.float32),
        jnp.ones((FF,), jnp.float32),
    )
    target_out, _ = forward(
        teacher_table, unpack(teacher_flat, False), token_ids, lengths, all_open
    )
    student_out, saved_acts = forward(table_rows, weights, token_ids, lengths, gate_set)
    student_low = student_out.astype(jnp.bfloat16)
    aligned = dense_mm(student_low, weights["w_align"])
    token_valid = saved_acts["key_valid"].reshape(-1)
    differ = aligned - target_out
    local_sum = jnp.sum(jnp.mean(differ * differ, axis=-1) * token_valid)
    global_sum = lax.psum(local_sum, "dp")
    d_aligned = (differ * (2.0 / D) * token_valid[:, None] / global_count).astype(jnp.bfloat16)
    d_w_align = jnp.einsum("td,te->de", student_low, d_aligned, preferred_element_type=jnp.float32)
    d_output = jnp.einsum(
        "te,de->td", d_aligned, weights["w_align"], preferred_element_type=jnp.float32
    )
    grad_map, d_embedded, gate_grads = backward(weights, saved_acts, gate_set, d_output)
    lag_value, lag_back = jax.vjp(lambda logit_in: lagrangian(logit_in, lagrange), mask_logodds)
    lag_weight = jnp.where(lax.axis_index("dp") == 0, 1.0, 0.0).astype(jnp.float32)
    d_logits = gate_back(jnp.concatenate(gate_grads))[0] + lag_back(lag_weight)[0]
    ordered = [
        grad_map["w_query"],
        grad_map["w_key"],
        grad_map["w_value"],
        grad_map["w_output"],
        d_w_align,
        grad_map["w_up"],
        grad_map["w_down"],
        grad_map["vectors"],
        grad_map["b_up"],
        d_logits,
    ]
    flat_parts = [piece.reshape(-1) for piece in ordered]
    filled = NPAR
    flat_term = jnp.concatenate(
        flat_parts + [jnp.zeros((flat_rows.shape[0] - filled,), jnp.float32)]
    )
    table_grad, flat_grad = (
        lax.psum_scatter(
            table_term(d_embedded, token_ids, table_rows.shape[0]),
            "dp",
            scatter_dimension=0,
            tiled=True,
        ),
        lax.psum_scatter(flat_term, "dp", scatter_dimension=0, tiled=True),
    )
    squares = jnp.sum(table_grad * table_grad) + jnp.sum(flat_grad * flat_grad)
    norm_squared = lax.psum(squares, "dp")
    grad_norm = jnp.sqrt(norm_squared)
    factor = jnp.minimum(1.0, clip_norm / (grad_norm + 1e-06))
    total_loss = global_sum / global_count + lag_value
    table_out, table_first_out, table_second_out = adam_step(
        word_table, table_first, table_second, table_grad * factor
    )
    flat_out, flat_first_out, flat_second_out = adam_step(
        layer_flat, flat_first, flat_second, flat_grad * factor
    )
    return (
        table_out,
        table_first_out,
        table_second_out,
        flat_out,
        flat_first_out,
        flat_second_out,
        total_loss,
        grad_norm,
    )


def solution(mesh):
    in_specs = (
        P("dp", None),
        P("dp"),
        P(),
        P(),
        P(),
        P(),
        P("dp", None),
        P("dp", None),
        P("dp", None),
        P("dp"),
        P("dp"),
        P("dp"),
    )
    out_specs = (P("dp", None), P("dp", None), P("dp", None), P("dp"), P("dp"), P("dp"), P(), P())
    return jax.shard_map(
        per_device, mesh=mesh, in_specs=in_specs, out_specs=out_specs, check_vma=False
    )
```

profile of v0, /device:TPU:0, one launch (start us, length us, event | category | flops | bytes accessed | tf_op | source)
XLA Modules:
  0.0 1322.3 jit_solution(11480576126675709873)
XLA Ops:
  13.1 42.2 %psum.21 = f32[]{:T(128)} all-reduce(f32[]{:T(128)S(6)} %convert_element_type.253), channel_id=1, replica_groups=mesh['dp'=32] {'dp'}, use_global_device_ids=true, to_apply=%region_21.22 | all-reduce | flops 1 | bytes 8 | tf_op jit(solution)/shard_map/psum | solution.py:333
  65.5 20.7 %gather_fusion.1 = bf16[4096,256]{1,0:T(8,128)(2,1)S(1)} fusion(bf16[31034,256]{1,0:T(8,128)(2,1)} %param.22, s32[4096]{0:T(1024)S(1)} %broadcast_clamp_fusion), kind=kCustom, calls=%fused_computation.1 | custom fusion | bytes 4210688 | tf_op jit(solution)/shard_map/jit(_take)/gather | solution.py:102
  98.3 12.7 reduce.26
  111.0 4.0 reshape.1202
  130.3 56.7 %all-gather.4.cloned.1.call-done = bf16[31232,256]{1,0:T(8,128)(2,1)} async-done(((bf16[976,256]{1,0:T(8,128)(2,1)}), bf16[31232,256]{1,0:T(8,128)(2,1)}) %all-gather.4.cloned.1.call-update) | async-done | bytes 15990800 | tf_op jit(solution)/shard_map/all_gather | solution.py:330
  188.0 20.8 %gather_fusion = bf16[4096,256]{1,0:T(8,128)(2,1)S(1)} fusion(bf16[31232,256]{1,0:T(8,128)(2,1)} %all-gather.4.cloned.1.call-done, s32[4096]{0:T(1024)S(1)} %broadcast_clamp_fusion.1), kind=kCustom, calls=%fused_computation | custom fusion | bytes 4210688 | tf_op jit(solution)/shard_map/jit(_take)/gather | solution.py:102
  210.8 3.5 multiply_reduce_fusion.18
  217.5 6.2 fusion.105
  225.8 3.2 reshape.1211
  229.1 7.1 copy.75
  238.2 7.1 reshape.1209
  245.2 6.9 copy.73
  254.2 7.1 reshape.1210
  261.3 5.6 copy.74
  266.9 4.2 convolution_convert_fusion
  271.1 7.5 reshape.1207
  278.6 6.9 copy.82
  285.6 4.2 fusion.96
  289.8 7.1 reshape.1205
  296.8 7.0 copy.80
  303.8 4.3 fusion.97
  308.1 7.1 reshape.1206
  315.2 6.9 copy.81
  322.1 51.9 %while.40 = (s32[]{:T(128)}, bf16[8,512,4,64]{1,3,2,0:T(8,128)(2,1)}, bf16[8,512,4,64]{1,3,2,0:T(8,128)(2,1)}, f32[8,512]{1,0:T(8,128)}, bf16[8,512,4,64]{1,3,2,0:T(8,128)(2,1)}, /*index=5*/bf16[8,512,4,64]{1,3,2,0:T(8,128)(2,1)}) while((s32[]{:T(128)}, bf16[8,512,4,64]{1,3,2,0:T(8,128)(2,1)}, ...), condition=%wide.region_15.16_spmd.clone, body=%wide.region_12.15_spmd.sunk.clone | while | flops 279968256 | bytes 13957201 | solution.py:167
  325.8 2.7 fusion.299
  332.3 2.7 fusion.299
  338.7 2.8 fusion.299
  345.2 2.8 fusion.299
  351.7 2.7 fusion.299
  358.1 2.8 fusion.299
  364.6 2.8 fusion.299
  371.1 2.8 fusion.299
  374.1 2.9 copy.83
  382.6 56.6 %while.39 = (s32[]{:T(128)}, f32[8,512,4,64]{1,3,2,0:T(8,128)}, f32[8,4,512]{2,1,0:T(4,128)}, bf16[8,512,4,64]{1,3,2,0:T(8,128)(2,1)}, f32[8,512]{1,0:T(8,128)},...) while((s32[]{:T(128)}, f32[8,512,4,64]{1,3,2,0:T(8,128)}, ...), condition=%wide.region_5.6_spmd.clone, body=%wide.region_2.0_spmd.sunk.clone | while | flops 279968256 | bytes 13965405 | solution.py:167
  386.8 2.8 fusion.296
  393.9 2.8 fusion.296
  401.0 2.8 fusion.296
  408.0 2.8 fusion.296
  415.1 2.8 fusion.296
  422.2 2.8 fusion.296
  429.3 2.8 fusion.296
  436.3 2.8 fusion.296
  439.2 3.6 multiply_convert_fusion.6
  445.1 41.1 %fusion.77.clone.1.clone.4 = bf16[4096,1024]{1,0:T(8,128)(2,1)S(1)} fusion(bf16[256,1024]{1,0:T(8,128)(2,1)S(1)} %copy-done.53, f32[1024]{0:T(1024)S(1)} %copy-done.90, f32[4096,256]{1,0:T(8,128)S(1)} %copy-done.23, f32[256]{0:T(256)S(1)} %copy-done.101, f32[256]{0:T(256)S(1)} %copy-done.102, f32[4096]{0:T(1024)S(1)} %add_rsqrt_fusion.1, ...), kind=kOutput, calls=%fused_computation.94.clone.clone.clone.clone.clone.1 | convolution fusion | flops 2429550592 | bytes 13146112 | tf_op jit(solution)/shard_map/dot_general | solution.py:93
  486.3 3.0 fusion.198
  491.0 4.4 fusion.189
  497.5 43.0 %multiply_convert_fusion.1 = (bf16[4096,1024]{1,0:T(8,128)(2,1)S(1)}, f32[4096,1024]{1,0:T(8,128)}, f32[4096,1024]{1,0:T(8,128)}) fusion(f32[1024]{0:T(1024)S(1)} %copy-done.92, f32[1024]{0:T(1024)S(1)} %copy-done.91, bf16[256,1024]{1,0:T(8,128)(2,1)S(1)} %copy-done.54, f32[4096,256]{1,0:T(8,128)S(1)} %get-tuple-element.290, f32[256]{0:T(256)S(1)} %copy-done.103, ...), kind=kOutput, calls=%fused_computation.111 | convolution fusion | flops 2433744896 | bytes 46704640 | tf_op jit(solution)/shard_map/dot_general | solution.py:93
  540.5 3.1 fusion.187
  547.4 3.9 multiply_reduce_fusion.2
  554.8 2.6 fusion.186
  561.8 19.4 %convert_reduce_fusion = (f32[1024]{0:T(1024)S(1)}, bf16[4096,1024]{1,0:T(8,128)(2,1)}, f32[1024]{0:T(1024)S(1)}) fusion(f32[4096,1024]{1,0:T(8,128)} %get-tuple-element.288, f32[1024]{0:T(1024)S(1)} %copy-done.92, f32[4096,1024]{1,0:T(8,128)} %get-tuple-element.350, f32[1024]{0:T(1024)S(1)} %copy-done.91, bf16[4096,256]{1,0:T(8,128)(2,1)S(1)} %get-tuple-element.276, ...), kind=kOutput, calls=%fused_computation.96 | convolution fusion | flops 2235561984 | bytes 44580864 | tf_op jit(solution)/shard_map/td,id->ti/dot_general | solution.py:215
  581.2 8.9 multiply_reduce_fusion.8
  590.8 4.4 convolution_bitcast_fusion.1
  604.6 110.4 %while.41 = (s32[]{:T(128)}, bf16[8,512,4,64]{1,3,2,0:T(8,128)(2,1)}, bf16[8,512,4,64]{1,3,2,0:T(8,128)(2,1)}, bf16[8,512,4,64]{1,3,2,0:T(8,128)(2,1)S(1)}, bf16...) while((s32[]{:T(128)}, ...), condition=%wide.region_28.29_spmd.clone, body=%wide.region_26.28_spmd.sunk.clone | while | flops 687471104 | bytes 34145396 | solution.py:237
  726.6 3.8 copy.123
  740.6 5.0 multiply_reduce_fusion.4
  749.0 29.8 %concatenate.40 = f32[860160]{0:T(1024)} concatenate(f32[65536]{0:T(1024)} %bitcast.353, f32[65536]{0:T(1024)} %bitcast.352, f32[65536]{0:T(1024)S(1)} %bitcast.351, f32[65536]{0:T(1024)S(1)} %bitcast.350, f32[65536]{0:T(1024)S(1)} %bitcast.349, f32[262144]{0:T(1024)} %bitcast.348, f32[262144]{0:T(1024)} %bitcast.347, f32[2560]{0:T(1024)S(1)} %reshape.1176, ...), dimensions={0} | concatenate | bytes 6881280 | tf_op jit(solution)/shard_map/concatenate | solution.py:376
  779.1 5.2 fusion.184
  786.6 2.6 reduce_sum.438
  789.2 39.3 %scatter_custom_fusion = f32[31232,256]{1,0:T(8,128)} fusion(s32[4608]{0:T(1024)S(1)} %fusion.125, f32[]{:T(128)} %constant.104.clone.1, f32[512,256]{1,0:T(8,128)S(1)} %reduce_sum.438, f32[]{:T(128)} %constant.294, f32[4096,256]{1,0:T(8,128)} %broadcast_add_fusion), kind=kCustom, calls=%fused_computation.127 | custom fusion | flops 2359296 | bytes 36700168 | tf_op jit(solution)/shard_map/scatter-add | solution.py:301
  830.0 85.7 %all-reduce.7.cloned.1.call-done = f32[860160]{0:T(1024)} async-done(((f32[860160]{0:T(1024)}), f32[860160]{0:T(1024)}) %all-reduce.7.cloned.1.call-update) | async-done | bytes 3440656
  917.3 338.7 %reduce-scatter.2.cloned.1.call-done = f32[976,256]{1,0:T(8,128)} async-done(((f32[31232,256]{1,0:T(8,128)}), f32[976,256]{1,0:T(8,128)}) %reduce-scatter.2.cloned.1.call-update) | async-done | bytes 999440 | tf_op jit(solution)/shard_map/reduce_scatter | solution.py:380
  1259.4 46.9 %all-reduce.4 = (f32[]{:T(128)}, f32[]{:T(128)}) all-reduce(f32[]{:T(128)S(6)} %add.582, f32[]{:T(128)} %select_reduce_fusion), channel_id=1, replica_groups=mesh['dp'=32] {'dp'}, use_global_device_ids=true, to_apply=%region_56.57 | all-reduce | flops 2 | bytes 16 | tf_op jit(solution)/shard_map/psum | solution.py:389
  1310.1 3.3 multiply_subtract_fusion
  (486 shorter events, 290.2 us)
Async XLA Ops:
  7.2 56.2 %copy-start.29 = (bf16[790016]{0:T(1024)(128)(2,1)S(1)}, bf16[790016]{0:T(1024)(128)(2,1)}, u32[]{:S(2)}) copy-start(bf16[790016]{0:T(1024)(128)(2,1)} %param.23) | copy-start | bytes 4740100
  7.2 91.2 %all-gather.6.cloned.1.call-start = ((), (), s32[]{:S(2)}) async-start(), calls=%async_computation.3 | async-start | bytes 3548160 | tf_op jit(solution)/shard_map/all_gather | solution.py:331
  9.0 178.0 %all-gather.4.cloned.1.call-start = ((), (), s32[]{:S(2)}) async-start(), calls=%async_computation.1 | async-start | bytes 16490496 | tf_op jit(solution)/shard_map/all_gather | solution.py:330
  11.1 904.6 %all-reduce.7.cloned.1.call-start = ((), (), s32[]{:S(2)}) async-start(), calls=%async_computation.4 | async-start | bytes 6881280
  58.1 7.4 copy-start.60
  59.4 37.1 %copy-start.71 = (pred[1,4,8,128]{3,1,2,0:T(4,128)(4,1)}, pred[1,4,8,128]{3,1,2,0:T(4,128)(4,1)S(1)}, u32[]{:S(2)}) copy-start(pred[1,4,8,128]{3,1,2,0:T(4,128)(4,1)S(1)} %copy.120) | copy-start | bytes 12292
  86.1 12.2 copy-start.13
  86.1 4.9 copy-start.97
  88.8 22.2 %copy-start.62 = (f32[4096]{0:T(1024)}, f32[4096]{0:T(1024)S(1)}, u32[]{:S(2)}) copy-start(f32[4096]{0:T(1024)S(1)} %broadcast_multiply_fusion.2) | copy-start | bytes 49156
  98.3 16.7 %copy-start.77 = (f32[1284]{0:T(1024)S(1)}, f32[1284]{0:T(1024)}, u32[]{:S(2)}) copy-start(f32[1284]{0:T(1024)} %param.20) | copy-start | bytes 15412
  115.0 71.9 %copy-start.26 = (bf16[860160]{0:T(1024)(128)(2,1)}, bf16[860160]{0:T(1024)(128)(2,1)S(1)}, u32[]{:S(2)}) copy-start(bf16[860160]{0:T(1024)(128)(2,1)S(1)} %reshape.1202) | copy-start | bytes 5160964
  125.0 98.8 %copy-start.32 = (bf16[256,256]{1,0:T(8,128)(2,1)}, bf16[256,256]{1,0:T(8,128)(2,1)S(1)}, u32[]{:S(2)}) copy-start(bf16[256,256]{1,0:T(8,128)(2,1)S(1)} %slice.317) | copy-start | bytes 393220
  125.1 127.1 %copy-start.34 = (bf16[256,256]{1,0:T(8,128)(2,1)}, bf16[256,256]{1,0:T(8,128)(2,1)S(1)}, u32[]{:S(2)}) copy-start(bf16[256,256]{1,0:T(8,128)(2,1)S(1)} %slice.314) | copy-start | bytes 393220
  125.1 111.0 %copy-start.30 = (bf16[256,256]{1,0:T(8,128)(2,1)}, bf16[256,256]{1,0:T(8,128)(2,1)S(1)}, u32[]{:S(2)}) copy-start(bf16[256,256]{1,0:T(8,128)(2,1)S(1)} %slice.311) | copy-start | bytes 393220
  188.0 29.6 %copy-start.10 = (f32[512,256]{1,0:T(8,128)}, f32[512,256]{1,0:T(8,128)S(1)}, u32[]{:S(2)}) copy-start(f32[512,256]{1,0:T(8,128)S(1)} %slice_convert_fusion) | copy-start | bytes 1572868
  208.8 15.0 %copy-start = (bf16[4096,256]{1,0:T(8,128)(2,1)}, bf16[4096,256]{1,0:T(8,128)(2,1)S(1)}, u32[]{:S(2)}) copy-start(bf16[4096,256]{1,0:T(8,128)(2,1)S(1)} %gather_fusion) | copy-start | bytes 6291460
  210.8 13.0 copy-start.40
  229.1 7.1 copy-start.5
  229.1 7.1 copy-start.85
  245.2 7.0 copy-start.84
  261.3 5.6 copy-start.51
  278.6 7.0 copy-start.50
  278.6 7.0 copy-start.94
  296.8 7.0 copy-start.49
  296.8 7.0 copy-start.93
  374.0 3.9 copy-start.3
  374.0 3.9 copy-start.46
  374.0 3.9 copy-start.87
  382.5 56.6 %copy-start.95 = (f32[4]{0:T(128)S(1)}, f32[4]{0:T(128)}, u32[]{:S(2)}) copy-start(f32[4]{0:T(128)} %slice.379) | copy-start | bytes 52
  439.1 4.9 copy-start.18
  444.9 45.8 %copy-start.15 = (bf16[32,8,8,512]{3,1,2,0:T(8,128)(2,1)}, bf16[32,8,8,512]{3,1,2,0:T(8,128)(2,1)S(1)}, u32[]{:S(2)}) copy-start(bf16[32,8,8,512]{3,1,2,0:T(8,128)(2,1)S(1)} %copy.117) | copy-start | bytes 6291460
  445.1 41.2 %copy-start.52 = (bf16[1024,256]{1,0:T(8,128)(2,1)S(1)}, bf16[1024,256]{1,0:T(8,128)(2,1)}, u32[]{:S(2)}) copy-start(bf16[1024,256]{1,0:T(8,128)(2,1)} %slice.355) | copy-start | bytes 1572868
  445.1 41.2 %copy-start.100 = (f32[256]{0:T(256)S(1)}, f32[256]{0:T(256)}, u32[]{:S(2)}) copy-start(f32[256]{0:T(256)} %get-tuple-element.327) | copy-start | bytes 3076
  495.4 45.1 %copy-start.8 = (f32[4096,256]{1,0:T(8,128)}, f32[4096,256]{1,0:T(8,128)S(1)}, u32[]{:S(2)}) copy-start(f32[4096,256]{1,0:T(8,128)S(1)} %get-tuple-element.290) | copy-start | bytes 12582916
  497.5 43.0 %copy-start.55 = (bf16[1024,256]{1,0:T(8,128)(2,1)S(1)}, bf16[1024,256]{1,0:T(8,128)(2,1)}, u32[]{:S(2)}) copy-start(bf16[1024,256]{1,0:T(8,128)(2,1)} %slice.329) | copy-start | bytes 1572868
  497.5 43.0 %copy-start.104 = (f32[256]{0:T(256)S(1)}, f32[256]{0:T(256)}, u32[]{:S(2)}) copy-start(f32[256]{0:T(256)} %get-tuple-element.337) | copy-start | bytes 3076
  545.0 2.4 copy-start.47
  545.0 2.4 copy-start.82
  545.0 2.4 copy-start.98
  545.0 2.4 copy-start.99
  581.2 8.9 copy-start.9
  581.2 9.6 copy-start.105
  590.8 4.4 copy-start.59
  595.2 2.6 copy-start.21
  597.8 3.1 copy-start.16
  599.9 2.4 copy-start.20
  599.9 2.4 copy-start.45
  599.9 2.4 copy-start.96
  715.0 2.9 copy-start.25
  718.2 3.7 copy-start.36
  718.2 4.9 copy-start.28
  726.6 4.8 copy-start.35
  734.5 2.9 copy-start.17
  740.6 7.6 copy-start.78
  740.6 8.4 copy-start.37
  749.0 29.9 %copy-start.61 = (s32[1,1,8,512]{3,1,2,0:T(1,128)S(1)}, s32[1,1,8,512]{3,1,2,0:T(1,128)}, u32[]{:S(2)}) copy-start(s32[1,1,8,512]{3,1,2,0:T(1,128)} %copy-done.60) | copy-start | bytes 49156
  749.0 30.0 %copy-start.63 = (f32[4096]{0:T(1024)S(1)}, f32[4096]{0:T(1024)}, u32[]{:S(2)}) copy-start(f32[4096]{0:T(1024)} %multiply_reduce_fusion.18) | copy-start | bytes 49156
  778.9 477.1 %reduce-scatter.2.cloned.1.call-start = ((), (), s32[]{:S(2)}) async-start(), calls=%async_computation.2 | async-start | bytes 32980992 | tf_op jit(solution)/shard_map/reduce_scatter | solution.py:380
  828.5 479.7 %copy-start.56 = (f32[26880]{0:T(1024)S(1)}, f32[26880]{0:T(1024)}, u32[]{:S(2)}) copy-start(f32[26880]{0:T(1024)} %param.27) | copy-start | bytes 322564
  828.5 479.7 %copy-start.64 = (f32[26880]{0:T(1024)S(1)}, f32[26880]{0:T(1024)}, u32[]{:S(2)}) copy-start(f32[26880]{0:T(1024)} %param.28) | copy-start | bytes 322564
  828.5 479.7 %copy-start.65 = (f32[26880]{0:T(1024)S(1)}, f32[26880]{0:T(1024)}, u32[]{:S(2)}) copy-start(f32[26880]{0:T(1024)} %param.29) | copy-start | bytes 322564
  828.5 481.5 %copy-start.27 = (f32[976,256]{1,0:T(8,128)S(1)}, f32[976,256]{1,0:T(8,128)}, u32[]{:S(2)}) copy-start(f32[976,256]{1,0:T(8,128)} %param.24) | copy-start | bytes 2998276
  828.6 481.5 %copy-start.38 = (f32[976,256]{1,0:T(8,128)S(1)}, f32[976,256]{1,0:T(8,128)}, u32[]{:S(2)}) copy-start(f32[976,256]{1,0:T(8,128)} %param.25) | copy-start | bytes 2998276
  828.6 481.5 %copy-start.39 = (f32[976,256]{1,0:T(8,128)S(1)}, f32[976,256]{1,0:T(8,128)}, u32[]{:S(2)}) copy-start(f32[976,256]{1,0:T(8,128)} %param.26) | copy-start | bytes 2998276
  (46 other events, 79.2 us)
Sparse Core Ops, SparseCore 0:
  11.4 62.5 all-gather.5
  76.8 110.0 all-gather.3
  779.0 136.6 all-reduce.6
  918.0 337.9 reduce-scatter.1
where the time goes:
time: 1340 us; the launch traced here: 1320 us
  waiting for transfers between devices  481 us (36%)
  matrix products  333 us (25%)
  local copies, waits for them, and re-layouts  216 us (16%)
  other arithmetic  175 us (13%)
  blocking collectives  89 us (7%)
  between operations  27 us (2%)
    reduce_scatter x1, waiting for transfers between devices, per_device(): lax.psum_scatter(table_term(d_embedded, token_ids, table_rows.shape[0]),...  339 us
    dot_general x13, matrix products, dense_mm(): return jnp.dot(left, right, preferred_element_type=jnp.float32)  117 us
    unnamed x5, waiting for transfers between devices  85.7 us
    all_gather x1, waiting for transfers between devices, per_device(): lax.all_gather(word_table.astype(jnp.bfloat16), 'dp', axis=0, tiled=True)  56.7 us
    psum x1, blocking collectives, per_device(): norm_squared = lax.psum(squares, 'dp')  46.9 us
    dot_general x16, matrix products, attend(): jnp.einsum('hqk,khd->qhd', shares_low, values, preferred_element_type=jnp...  44.6 us
    psum x1, blocking collectives, per_device(): global_count = lax.psum(jnp.sum(lengths).astype(jnp.float32), 'dp')  42.2 us
    gather x2, local copies, waits for them, and re-layouts, embed_tokens(): jnp.take(table_rows, token_ids.reshape(-1), axis=0).astype(jnp.float32)  41.4 us
  transfers between devices with their start and end apart: 4, of which 3 were waited for; matrix products, arithmetic and copies ran while one was open for 9% of the time, Pallas kernels for 0%

commit v1 on v0

v1 whole, which is shorter than its diff:
```python
import functools
import math

import jax
import jax.numpy as jnp
from jax import lax
from jax.experimental import pallas as pl
from jax.experimental.pallas import tpu as pltpu
from jax.sharding import PartitionSpec as P

D = 256
HEADS = 4
HD = D // HEADS
FF = 1024
LEN = 512
VOCAB = 30522
NPAR = 856836
LANES = 128
norm_eps = 1e-12
f32 = jnp.float32
bf16 = jnp.bfloat16
VMEM_LIMIT = 56 * 2**20

C_GH = 10 * D
C_HEAD = 11 * D
C_BUP = 12 * D
C_GI = 12 * D + FF
C_ROWS = 12 * D + 2 * FF
A_BUP = 10 * D
A_GH = 10 * D + FF
A_HEAD = 11 * D + FF
A_GI = 12 * D + FF
A_ROWS = 12 * D + 2 * FF
R_UP = 5 * 512
R_DOWN = R_UP + 2048
R_VEC = R_DOWN + 2048
R_BUP = R_VEC + 20
R_LOGIT = R_BUP + 8
R_USED = R_LOGIT + 11


def nn(left, right):
    return jnp.dot(left, right, preferred_element_type=f32)


def nt(left, right):
    return lax.dot_general(left, right, (((1,), (1,)), ((), ())), preferred_element_type=f32)


def chunks(span):
    return [(c, min(256, span - c)) for c in range(0, span, 256)]


def wide(col_ref, row, rows, width):
    col = col_ref[row : row + rows, :]
    return jnp.concatenate([col] * (width // LANES), axis=1) if width > LANES else col


def lanes_in(values):
    total = values[:, :LANES]
    for c in range(LANES, values.shape[1], LANES):
        total = total + values[:, c : c + LANES]
    return total


def eye(size):
    return (
        lax.broadcasted_iota(jnp.int32, (size, size), 0)
        == lax.broadcasted_iota(jnp.int32, (size, size), 1)
    ).astype(bf16)


def standardise(x):
    mean = jnp.sum(x, axis=0, keepdims=True) * (1.0 / D)
    centred = x - mean
    variance = jnp.sum(centred * centred, axis=0, keepdims=True) * (1.0 / D)
    scale = lax.rsqrt(variance + norm_eps)
    return centred * scale, scale


def standardise_back(dx, hat, scale):
    mean_one = jnp.sum(dx, axis=0, keepdims=True) * (1.0 / D)
    mean_two = jnp.sum(dx * hat, axis=0, keepdims=True) * (1.0 / D)
    return scale * (dx - mean_one - hat * mean_two)


def gelu_parts(x):
    half_erf = 0.5 * lax.erf(x * (2.0**-0.5)) + 0.5
    return half_erf


def forward_body(span, offset, length, student, rows_ref, pos_ref, col_ref, w, sc, eyes):
    for c, width in chunks(span):
        tokens = rows_ref[pl.ds(offset + c, width), :]
        embedded = nt(eyes[D], tokens) + pos_ref[:, c : c + width]
        hat, scale = standardise(embedded)
        start = hat * wide(col_ref, 0, D, width) + wide(col_ref, D, D, width)
        if student:
            sc["hat0"][:, c : c + width] = hat
            sc["scale"][0:1, c : c + width] = scale
            start = start * wide(col_ref, C_GH, D, width)
        sc["start"][:, c : c + width] = start
        start_low = start.astype(bf16)
        sc["start_low"][:, c : c + width] = start_low
        factor = HD**-0.5
        q = nn(w["qkvT"][0:D, :], start_low) + wide(col_ref, 6 * D, D, width)
        sc["qkv"][0:D, c : c + width] = q.astype(bf16)
        k = nn(w["qkvT"][D : 2 * D, :], start_low).astype(bf16)
        sc["qkv"][D : 2 * D, c : c + width] = k
        v = (nn(w["qkvT"][2 * D : 3 * D, :], start_low) + wide(col_ref, 7 * D, D, width)).astype(
            bf16
        )
        sc["qkv"][2 * D : 3 * D, c : c + width] = v
        for h in range(HEADS):
            sc["k_rows"][h, c : c + width, :] = nt(eyes[width], k[h * HD : (h + 1) * HD, :]).astype(
                bf16
            )
            if student:
                sc["v_rows"][h, c : c + width, :] = nt(
                    eyes[width], v[h * HD : (h + 1) * HD, :]
                ).astype(bf16)
    for c, width in chunks(span):
        valid = lax.broadcasted_iota(jnp.int32, (span, width), 0) < length
        for h in range(HEADS):
            q_h = sc["qkv"][h * HD : (h + 1) * HD, c : c + width] * bf16(HD**-0.5)
            scores = jnp.where(valid, nn(sc["k_rows"][h, 0:span, :], q_h), -1e30)
            shares = jnp.exp(scores - jnp.max(scores, axis=0, keepdims=True))
            shares_low = (shares * (1.0 / jnp.sum(shares, axis=0, keepdims=True))).astype(bf16)
            if student:
                sc["shares"][h, 0:span, c : c + width] = shares_low
            context = nn(sc["qkv"][2 * D + h * HD : 2 * D + (h + 1) * HD, 0:span], shares_low)
            if student:
                sc["context"][h * HD : (h + 1) * HD, c : c + width] = context
                context = context * wide(col_ref, C_HEAD + h * HD, HD, width)
            sc["gated"][h * HD : (h + 1) * HD, c : c + width] = context.astype(bf16)
    for c, width in chunks(span):
        branch = nn(w["oT"][...], sc["gated"][:, c : c + width]) + wide(col_ref, 8 * D, D, width)
        if student:
            sc["branch"][:, c : c + width] = branch
            branch = branch * wide(col_ref, C_GH, D, width)
        hat, scale = standardise(sc["start"][:, c : c + width] + branch)
        middle = hat * wide(col_ref, 2 * D, D, width) + wide(col_ref, 3 * D, D, width)
        if student:
            sc["hat1"][:, c : c + width] = hat
            sc["scale"][1:2, c : c + width] = scale
        middle_low = middle.astype(bf16)
        if student:
            sc["middle_low"][:, c : c + width] = middle_low
        for r in range(0, FF, D):
            pre = nn(w["upT"][r : r + D, :], middle_low) + wide(col_ref, C_BUP + r, D, width)
            cdf = 0.5 * lax.erf(pre * (2.0**-0.5)) + 0.5
            act = pre * cdf
            if student:
                inner = wide(col_ref, C_GI + r, D, width)
                pdf = jnp.exp(pre * pre * -0.5) * (1.0 / math.sqrt(2.0 * math.pi))
                sc["act"][r : r + D, c : c + width] = act
                sc["slope"][r : r + D, c : c + width] = (cdf + pre * pdf) * inner
                act = act * inner
            sc["up"][r : r + D, c : c + width] = act.astype(bf16)
        down = nn(w["downT"][...], sc["up"][:, c : c + width]) + wide(col_ref, 9 * D, D, width)
        if student:
            sc["down"][:, c : c + width] = down
            down = down * wide(col_ref, C_GH, D, width)
        hat, scale = standardise(middle + down)
        out = hat * wide(col_ref, 4 * D, D, width) + wide(col_ref, 5 * D, D, width)
        if student:
            sc["hat2"][:, c : c + width] = hat
            sc["scale"][2:3, c : c + width] = scale
        sc["out"][:, c : c + width] = out


def backward_body(span, length, factor, target_ref, col_ref, w, sc, acc, add_ref, loss_ref, grad_ref, pos_add):
    def add(row, values):
        add_ref[row : row + values.shape[0], :] += lanes_in(values)

    for c, width in chunks(span):
        cols = slice(c, c + width)
        out_low = sc["out"][:, cols].astype(bf16)
        sc["out_low"][:, cols] = out_low
        differ = nn(w["aT"][...], out_low) - target_ref[0, :, cols]
        token_valid = (lax.broadcasted_iota(jnp.int32, (1, width), 1) + c < length).astype(f32)
        loss_ref[0:1, cols] += (
            jnp.sum(differ * differ, axis=0, keepdims=True) * (1.0 / D) * token_valid
        )
        d_aligned = (differ * (token_valid * factor)).astype(bf16)
        sc["d_aligned"][:, cols] = d_aligned
        d_out = nn(w["a"][...], d_aligned)
        hat = sc["hat2"][:, cols]
        add(4 * D, d_out * hat)
        add(5 * D, d_out)
        d_second = standardise_back(d_out * wide(col_ref, 4 * D, D, width), hat, sc["scale"][2:3, cols])
        add(A_GH, d_second * sc["down"][:, cols])
        d_down = (d_second * wide(col_ref, C_GH, D, width)).astype(bf16)
        sc["d_down"][:, cols] = d_down
        add(9 * D, d_down.astype(f32))
        for r in range(0, FF, D):
            d_up = nn(w["down"][r : r + D, :], d_down)
            add(A_GI + r, d_up * sc["act"][r : r + D, cols])
            d_pre = (d_up * sc["slope"][r : r + D, cols]).astype(bf16)
            sc["d_pre"][r : r + D, cols] = d_pre
            add(A_BUP + r, d_pre.astype(f32))
        d_middle = d_second + nn(w["up"][...], sc["d_pre"][:, cols])
        hat = sc["hat1"][:, cols]
        add(2 * D, d_middle * hat)
        add(3 * D, d_middle)
        d_first = standardise_back(
            d_middle * wide(col_ref, 2 * D, D, width), hat, sc["scale"][1:2, cols]
        )
        sc["d_first"][:, cols] = d_first
        add(A_GH, d_first * sc["branch"][:, cols])
        d_branch = (d_first * wide(col_ref, C_GH, D, width)).astype(bf16)
        sc["d_branch"][:, cols] = d_branch
        add(8 * D, d_branch.astype(f32))
        d_gated = nn(w["o"][...], d_branch)
        context = sc["context"][:, cols]
        add(A_HEAD, d_gated * context)
        d_context = d_gated * wide(col_ref, C_HEAD, D, width)
        sc["d_context"][:, cols] = d_context.astype(bf16)
        dot_rows = d_context * context
        for h in range(HEADS):
            sc["delta"][h : h + 1, cols] = jnp.sum(
                dot_rows[h * HD : (h + 1) * HD, :], axis=0, keepdims=True
            )
    full = slice(0, span)
    acc["a"][...] += nt(sc["out_low"][:, full], sc["d_aligned"][:, full])
    acc["down"][...] += nt(sc["up"][:, full], sc["d_down"][:, full])
    acc["up"][...] += nt(sc["middle_low"][:, full], sc["d_pre"][:, full])
    acc["o"][...] += nt(sc["gated"][:, full], sc["d_branch"][:, full])
    for h in range(HEADS):
        rows = slice(h * HD, (h + 1) * HD)
        d_value = nt(sc["d_context"][rows, full], sc["shares"][h, 0:span, 0:span])
        sc["d_qkv"][2 * D + h * HD : 2 * D + (h + 1) * HD, full] = d_value.astype(bf16)
        d_key = None
        for c, width in chunks(span):
            cols = slice(c, c + width)
            d_shares = nn(sc["v_rows"][h, 0:span, :], sc["d_context"][rows, cols])
            d_scores = (
                sc["shares"][h, 0:span, cols].astype(f32) * (d_shares - sc["delta"][h : h + 1, cols])
            ).astype(bf16)
            sc["d_qkv"][rows, cols] = (
                nn(sc["qkv"][D + h * HD : D + (h + 1) * HD, full], d_scores) * (HD**-0.5)
            ).astype(bf16)
            part = nt(sc["qkv"][rows, cols], d_scores)
            d_key = part if d_key is None else d_key + part
        sc["d_qkv"][D + h * HD : D + (h + 1) * HD, full] = (d_key * (HD**-0.5)).astype(bf16)
    acc["qkv"][...] += nt(sc["start_low"][:, full], sc["d_qkv"][:, full])
    for c, width in chunks(span):
        cols = slice(c, c + width)
        add(6 * D, sc["d_qkv"][0:D, cols].astype(f32))
        add(7 * D, sc["d_qkv"][2 * D : 3 * D, cols].astype(f32))
        d_start = sc["d_first"][:, cols] + nn(w["qkv"][...], sc["d_qkv"][:, cols])
        hat = sc["hat0"][:, cols]
        gain = wide(col_ref, 0, D, width)
        add(A_GH, d_start * (hat * gain + wide(col_ref, D, D, width)))
        d_norm = d_start * wide(col_ref, C_GH, D, width)
        add(0, d_norm * hat)
        add(D, d_norm)
        d_embedded = standardise_back(d_norm * gain, hat, sc["scale"][0:1, cols])
        pos_add[:, cols] += d_embedded
        grad_ref[0, :, cols] = d_embedded.astype(bf16)
    if span < LEN:
        grad_ref[0, :, span:LEN] = jnp.zeros((D, LEN - span), bf16)


SPANS = (256, 384, 512)


def by_span(length, body):
    for i, span in enumerate(SPANS):
        low = SPANS[i - 1] if i else 0
        test = length > low
        if i == 0:
            test = length <= span
        elif i < len(SPANS) - 1:
            test = (length > low) & (length <= span)
        pl.when(test)(functools.partial(body, span))


def set_up(pos_in, pos_ref, eyes_refs):
    for size, ref in eyes_refs.items():
        ref[...] = eye(size)
    for c in range(0, LEN, 256):
        pos_ref[:, c : c + 256] = nt(eyes_refs[256][...], pos_in[c : c + 256, :])


TEACHER_W = (("qkvT", (3 * D, D)), ("oT", (D, D)), ("upT", (FF, D)), ("downT", (D, FF)))
STUDENT_W = TEACHER_W + (
    ("aT", (D, D)),
    ("qkv", (D, 3 * D)),
    ("o", (D, D)),
    ("a", (D, D)),
    ("up", (D, FF)),
    ("down", (FF, D)),
)
TEACHER_S = (
    ("start", (D, LEN), f32),
    ("start_low", (D, LEN), bf16),
    ("qkv", (3 * D, LEN), bf16),
    ("k_rows", (HEADS, LEN, HD), bf16),
    ("gated", (D, LEN), bf16),
    ("up", (FF, LEN), bf16),
)
STUDENT_S = TEACHER_S + (
    ("hat0", (D, LEN), f32),
    ("hat1", (D, LEN), f32),
    ("hat2", (D, LEN), f32),
    ("scale", (8, LEN), f32),
    ("v_rows", (HEADS, LEN, HD), bf16),
    ("shares", (HEADS, LEN, LEN), bf16),
    ("context", (D, LEN), f32),
    ("branch", (D, LEN), f32),
    ("middle_low", (D, LEN), bf16),
    ("act", (FF, LEN), f32),
    ("slope", (FF, LEN), f32),
    ("down", (D, LEN), f32),
    ("out", (D, LEN), f32),
    ("out_low", (D, LEN), bf16),
    ("d_aligned", (D, LEN), bf16),
    ("d_down", (D, LEN), bf16),
    ("d_pre", (FF, LEN), bf16),
    ("d_first", (D, LEN), f32),
    ("d_branch", (D, LEN), bf16),
    ("d_context", (D, LEN), bf16),
    ("delta", (8, LEN), f32),
    ("d_qkv", (3 * D, LEN), bf16),
)
ACCS = (
    ("qkv", (D, 3 * D)),
    ("o", (D, D)),
    ("a", (D, D)),
    ("up", (D, FF)),
    ("down", (FF, D)),
)


def teacher_kernel(len_ref, off_ref, rows_ref, pos_in, col_ref, *rest):
    w = {name: rest[i] for i, (name, _) in enumerate(TEACHER_W)}
    out_ref = rest[len(TEACHER_W)]
    scratch = rest[len(TEACHER_W) + 1 :]
    sc = {entry[0]: scratch[i] for i, entry in enumerate(TEACHER_S)}
    pos_ref, eye_one, eye_two = scratch[len(TEACHER_S) :]
    s = pl.program_id(0)
    sc["out"] = out_ref.at[0]

    @pl.when(s == 0)
    def _():
        set_up(pos_in, pos_ref, {128: eye_one, 256: eye_two})

    eyes = {128: eye_one, 256: eye_two}

    class Read:
        def __getitem__(self, size):
            return eyes[size][...]

    length = len_ref[s]

    def body(span):
        offset = pl.multiple_of(off_ref[s], 16)
        forward_body(span, offset, length, False, rows_ref, pos_ref, col_ref, w, sc, Read())

    by_span(length, body)


def student_kernel(len_ref, off_ref, fac_ref, rows_ref, pos_in, target_ref, col_ref, slope_in, lag_in, *rest):
    w = {name: rest[i] for i, (name, _) in enumerate(STUDENT_W)}
    rest = rest[len(STUDENT_W) :]
    flat_ref, grad_ref, pos_add, loss_ref = rest[:4]
    scratch = rest[4:]
    sc = {entry[0]: scratch[i] for i, entry in enumerate(STUDENT_S)}
    scratch = scratch[len(STUDENT_S) :]
    acc = {entry[0]: scratch[i] for i, entry in enumerate(ACCS)}
    add_ref, pos_ref, eye_one, eye_two = scratch[len(ACCS) :]
    s = pl.program_id(0)

    @pl.when(s == 0)
    def _():
        set_up(pos_in, pos_ref, {128: eye_one, 256: eye_two})
        for ref in list(acc.values()) + [add_ref, pos_add, loss_ref]:
            ref[...] = jnp.zeros(ref.shape, f32)

    eyes = {128: eye_one, 256: eye_two}

    class Read:
        def __getitem__(self, size):
            return eyes[size][...]

    length = len_ref[s]

    def body(span):
        offset = pl.multiple_of(off_ref[s], 16)
        forward_body(span, offset, length, True, rows_ref, pos_ref, col_ref, w, sc, Read())
        backward_body(
            span, length, fac_ref[0], target_ref, col_ref, w, sc, acc, add_ref, loss_ref, grad_ref, pos_add
        )

    by_span(length, body)

    @pl.when(s == pl.num_programs(0) - 1)
    def _():
        for i in range(3):
            for j in range(2):
                at = i * D + j * LANES
                flat_ref[pl.ds(512 * i + j, D, stride=2), :] = acc["qkv"][:, at : at + LANES]
        for j in range(2):
            lanes = slice(j * LANES, (j + 1) * LANES)
            flat_ref[pl.ds(512 * 3 + j, D, stride=2), :] = acc["o"][:, lanes]
            flat_ref[pl.ds(512 * 4 + j, D, stride=2), :] = acc["a"][:, lanes]
            flat_ref[pl.ds(R_DOWN + j, FF, stride=2), :] = acc["down"][:, lanes]
        for j in range(8):
            flat_ref[pl.ds(R_UP + j, D, stride=8), :] = acc["up"][:, j * LANES : (j + 1) * LANES]
        ones = jnp.ones((8, LANES), f32)

        def summed(row, rows):
            return lax.dot_general(
                ones,
                add_ref[row : row + rows, :],
                (((1,), (1,)), ((), ())),
                preferred_element_type=f32,
                precision=lax.Precision.HIGHEST,
            )

        for i in range(10):
            sums = summed(i * D, D)
            for j in range(2):
                flat_ref[R_VEC + 2 * i + j : R_VEC + 2 * i + j + 1, :] = sums[
                    0:1, j * LANES : (j + 1) * LANES
                ]
        sums = summed(A_BUP, FF)
        for j in range(8):
            flat_ref[R_BUP + j : R_BUP + j + 1, :] = sums[0:1, j * LANES : (j + 1) * LANES]
        hidden = summed(A_GH, D)
        group = (
            lax.broadcasted_iota(jnp.int32, (D, LANES), 0) // HD
            == lax.broadcasted_iota(jnp.int32, (D, LANES), 1)
        ).astype(f32)
        heads = jnp.dot(
            summed(A_HEAD, D), group, preferred_element_type=f32, precision=lax.Precision.HIGHEST
        )
        inner = summed(A_GI, FF)
        moved = pltpu.roll(jnp.concatenate([inner, jnp.zeros((8, LANES), f32)], axis=1), HEADS, 1)
        lane = lax.broadcasted_iota(jnp.int32, (8, LANES), 1)
        first = jnp.where(lane < HEADS, heads, moved[:, :LANES])
        tail = [hidden[:, :LANES], hidden[:, LANES:], first] + [
            moved[:, j * LANES : (j + 1) * LANES] for j in range(1, 9)
        ]
        for j, piece in enumerate(tail):
            flat_ref[R_LOGIT + j : R_LOGIT + j + 1, :] = (
                piece[0:1] * slope_in[j : j + 1, :] + lag_in[j : j + 1, :]
            )
        flat_ref[R_USED:, :] = jnp.zeros((flat_ref.shape[0] - R_USED, LANES), f32)


def whole_spec():
    return pl.BlockSpec(memory_space=pltpu.VMEM)


def smem_spec():
    return pl.BlockSpec(memory_space=pltpu.SMEM)


def seq_spec():
    return pl.BlockSpec((1, D, LEN), lambda s: (s, 0, 0))


def extra_scratch():
    return [
        pltpu.VMEM((D, LEN), f32),
        pltpu.VMEM((128, 128), bf16),
        pltpu.VMEM((256, 256), bf16),
    ]


def run_teacher(lengths, offsets, rows, places, columns, weights):
    seqs = lengths.shape[0]
    return pl.pallas_call(
        teacher_kernel,
        grid=(seqs,),
        out_shape=jax.ShapeDtypeStruct((seqs, D, LEN), f32),
        in_specs=[smem_spec(), smem_spec()] + [whole_spec()] * (3 + len(TEACHER_W)),
        out_specs=seq_spec(),
        scratch_shapes=[pltpu.VMEM(shape, kind) for _, shape, kind in TEACHER_S] + extra_scratch(),
        compiler_params=pltpu.CompilerParams(vmem_limit_bytes=VMEM_LIMIT),
        name="teacher",
    )(lengths, offsets, rows, places, columns, *[weights[name] for name, _ in TEACHER_W])


def run_student(lengths, offsets, factor, rows, places, target, columns, slopes, lag, weights, flat_rows):
    seqs = lengths.shape[0]
    return pl.pallas_call(
        student_kernel,
        grid=(seqs,),
        out_shape=(
            jax.ShapeDtypeStruct((flat_rows, LANES), f32),
            jax.ShapeDtypeStruct((seqs, D, LEN), bf16),
            jax.ShapeDtypeStruct((D, LEN), f32),
            jax.ShapeDtypeStruct((8, LEN), f32),
        ),
        in_specs=[smem_spec()] * 3
        + [whole_spec()] * 2
        + [seq_spec()]
        + [whole_spec()] * (3 + len(STUDENT_W)),
        out_specs=(
            pl.BlockSpec((flat_rows, LANES), lambda s: (0, 0)),
            seq_spec(),
            pl.BlockSpec((D, LEN), lambda s: (0, 0)),
            pl.BlockSpec((8, LEN), lambda s: (0, 0)),
        ),
        scratch_shapes=[pltpu.VMEM(shape, kind) for _, shape, kind in STUDENT_S]
        + [pltpu.VMEM(shape, f32) for _, shape in ACCS]
        + [pltpu.VMEM((A_ROWS, LANES), f32)]
        + extra_scratch(),
        compiler_params=pltpu.CompilerParams(vmem_limit_bytes=VMEM_LIMIT),
        name="student",
    )(
        lengths,
        offsets,
        factor,
        rows,
        places,
        target,
        columns,
        slopes,
        lag,
        *[weights[name] for name, _ in STUDENT_W],
    )


clip_norm = 0.002
learn_rate = 0.015
beta_one = 0.9
beta_two = 0.999
adam_eps = 1e-08
decay_rate = 0.01
sparse_target = 0.3
ADAM_STEP = 10
relaxation_heat = 2.0 / 3.0
widened_left_limit = -0.1
widened_right_limit = 1.1


def layout(student):
    square = (D, D)
    entries = [("w_query", square), ("w_key", square), ("w_value", square), ("w_output", square)]
    if student:
        entries = entries + [("w_align", square)]
    entries = entries + [
        ("w_up", (D, FF)),
        ("w_down", (FF, D)),
        ("vectors", (10, D)),
        ("b_up", (FF,)),
    ]
    if student:
        entries = entries + [("gate_logits", (D + HEADS + FF,))]
    return entries


def unpack(flat_vector, student):
    pieces = {}
    offset = 0
    for entry_name, entry_shape in layout(student):
        length = math.prod(entry_shape)
        pieces[entry_name] = flat_vector[offset : offset + length].reshape(entry_shape)
        offset = offset + length
    return pieces


def gate_values(mask_logodds, flat_random_sample):
    logistic_function = jax.nn.sigmoid(
        (jnp.log(flat_random_sample) - jnp.log(1.0 - flat_random_sample) + mask_logodds)
        / relaxation_heat
    )
    return jnp.clip(
        logistic_function * (widened_right_limit - widened_left_limit) + widened_left_limit,
        0.0,
        1.0,
    )


def lagrangian(mask_logodds, lagrange):
    survival_probability = jax.nn.sigmoid(
        mask_logodds - relaxation_heat * math.log(-widened_left_limit / widened_right_limit)
    )
    kept_hidden = jnp.mean(survival_probability[:D])
    kept_rest = 4.0 * HD * jnp.sum(survival_probability[D : D + HEADS]) + 2.0 * jnp.sum(
        survival_probability[D + HEADS :]
    )
    expected = kept_hidden * kept_rest / (4.0 * D + 2.0 * FF)
    excess = expected - sparse_target
    return lagrange[0] * excess + lagrange[1] * excess * excess


def adam_step(weight, first_old, second, clipped):
    first_new = beta_one * first_old + (1.0 - beta_one) * clipped
    second_new = beta_two * second + (1.0 - beta_two) * clipped * clipped
    first_hat = first_new / (1.0 - beta_one**ADAM_STEP)
    second_hat = second_new / (1.0 - beta_two**ADAM_STEP)
    weight_new = weight - learn_rate * (
        first_hat / (jnp.sqrt(second_hat) + adam_eps) + decay_rate * weight
    )
    return (weight_new, first_new, second_new)


def kernel_weights(pieces, student):
    w = {}
    w["qkv"] = jnp.concatenate([pieces["w_query"], pieces["w_key"], pieces["w_value"]], axis=1)
    w["qkvT"] = w["qkv"].T
    for name, source in (("o", "w_output"), ("up", "w_up"), ("down", "w_down")):
        w[name] = pieces[source]
        w[name + "T"] = pieces[source].T
    if student:
        w["a"] = pieces["w_align"]
        w["aT"] = w["a"].T
    return w


def columns_of(pieces, gates=None):
    vectors = pieces["vectors"].astype(f32).reshape(-1)
    bias = pieces["b_up"].astype(f32)
    if gates is None:
        gates = jnp.ones((D + HEADS + FF,), f32)
    parts = [vectors, gates[:D], jnp.repeat(gates[D : D + HEADS], HD), bias, gates[D + HEADS :]]
    column = jnp.concatenate(parts)
    return jnp.broadcast_to(column[:, None], (column.shape[0], LANES))


def pad_rows(values):
    return jnp.pad(values, (0, 16 * LANES - values.shape[0])).reshape(16, LANES)


def per_device(
    devices,
    token_ids,
    lengths,
    gate_noise,
    lagrange,
    teacher_table,
    teacher_flat,
    word_table,
    table_first,
    table_second,
    layer_flat,
    flat_first,
    flat_second,
):
    seqs = token_ids.shape[0]
    half = seqs // 2
    mates = [(i, devices - 1 - i) for i in range(devices)]
    sent = jnp.concatenate(
        [token_ids[half:], jnp.pad(lengths[half:], (0, LEN - half)).reshape(1, LEN)]
    )
    got = lax.ppermute(sent, "dp", mates)
    ids = jnp.concatenate([token_ids[:half], got[:half]])
    lens = jnp.concatenate([lengths[:half], got[half, :half]])
    offsets = jnp.arange(seqs, dtype=jnp.int32) * LEN

    table_rows = lax.all_gather(word_table.astype(bf16), "dp", axis=0, tiled=True)
    flat_rows = lax.all_gather(layer_flat.astype(bf16), "dp", axis=0, tiled=True)
    global_count = lax.psum(jnp.sum(lengths).astype(f32), "dp")
    factor = ((2.0 / D) / global_count).reshape(1)

    teacher = unpack(teacher_flat, False)
    target = run_teacher(
        lens,
        offsets,
        jnp.take(teacher_table, ids.reshape(-1), axis=0),
        teacher_table[VOCAB : VOCAB + LEN],
        columns_of(teacher),
        kernel_weights(teacher, False),
    )

    pieces = unpack(flat_rows, True)
    logits = pieces["gate_logits"].astype(f32)
    gates, gate_back = jax.vjp(lambda x: gate_values(x, gate_noise), logits)
    slopes = gate_back(jnp.ones_like(gates))[0]
    lag_value, lag_back = jax.vjp(lambda x: lagrangian(x, lagrange), logits)
    lag_weight = jnp.where(lax.axis_index("dp") == 0, 1.0, 0.0).astype(f32)
    flat_term, grad_rows, place_grad, loss_rows = run_student(
        lens,
        offsets,
        factor,
        jnp.take(table_rows, ids.reshape(-1), axis=0),
        table_rows[VOCAB : VOCAB + LEN],
        target,
        columns_of(pieces, gates),
        pad_rows(slopes),
        pad_rows(lag_back(lag_weight)[0]),
        kernel_weights(pieces, True),
        flat_rows.shape[0] // LANES,
    )
    global_sum = lax.psum(jnp.sum(loss_rows), "dp")
    updates = jnp.transpose(grad_rows, (0, 2, 1)).reshape(seqs * LEN, D).astype(f32)
    index = jnp.concatenate([ids.reshape(-1), VOCAB + jnp.arange(LEN, dtype=jnp.int32)])
    updates = jnp.concatenate([updates, place_grad.T])
    table_term = jnp.zeros((table_rows.shape[0], D), f32).at[index].add(updates)
    table_grad = lax.psum_scatter(table_term, "dp", scatter_dimension=0, tiled=True)
    flat_grad = lax.psum_scatter(flat_term.reshape(-1), "dp", scatter_dimension=0, tiled=True)
    squares = jnp.sum(table_grad * table_grad) + jnp.sum(flat_grad * flat_grad)
    grad_norm = jnp.sqrt(lax.psum(squares, "dp"))
    clip = jnp.minimum(1.0, clip_norm / (grad_norm + 1e-06))
    total_loss = global_sum / global_count + lag_value
    table_new = adam_step(word_table, table_first, table_second, table_grad * clip)
    flat_new = adam_step(layer_flat, flat_first, flat_second, flat_grad * clip)
    return (*table_new, *flat_new, total_loss, grad_norm)


def solution(mesh):
    row, flat, copied = P("dp", None), P("dp"), P()
    in_specs = (row, flat, copied, copied, copied, copied, row, row, row, flat, flat, flat)
    out_specs = (row, row, row, flat, flat, flat, copied, copied)
    return jax.shard_map(
        functools.partial(per_device, mesh.shape["dp"]),
        mesh=mesh,
        in_specs=in_specs,
        out_specs=out_specs,
        check_vma=False,
    )
```

time: 1340 us -> 878 us (0.66); the launches traced: 1320 us -> 874 us
  matrix products: 333 us -> 0 us
  local copies, waits for them, and re-layouts: 216 us -> 76.9 us
  Pallas kernels: 0 us -> 135 us
  other arithmetic: 175 us -> 75.3 us
    dot_general x99 -> x0, matrix products: 333 us -> none  [the longest x13 117 us: dense_mm(): return jnp.dot(left, right, preferred_element_type=jnp.float32)]
    pallas_call x0 -> x2, Pallas kernels: none -> 135 us  [the longest x1 95 us: run_student(): pl.pallas_call(student_kernel, grid=(seqs,), out_shape=(jax.ShapeDtypeStr...]
    while x9 -> x0, local copies, waits for them, and re-layouts: 45.3 us -> none  [the longest x6 40.4 us: forward(): lax.map(lambda group_in: attend(*group_in), (queries, keys_low, values, k...]
    reduce_sum x34 -> x2, other arithmetic: 46.3 us -> 1.23 us  [the longest x1 0.63 us: per_device(): global_count = lax.psum(jnp.sum(lengths).astype(f32), 'dp')]
    reshape x7 -> x2, local copies, waits for them, and re-layouts: 39 us -> 0.69 us  [the longest x1 0.6 us: pad_rows(): return jnp.pad(values, (0, 16 * LANES - values.shape[0])).reshape(16, LANES)]
    all_gather x2, waiting for transfers between devices: 56.7 us -> 25.1 us  [the longest x1 25.1 us: per_device(): lax.all_gather(word_table.astype(bf16), 'dp', axis=0, tiled=True)]
    concatenate x2 -> x3, local copies, waits for them, and re-layouts: 29.9 us -> 0.08 us  [the longest x2 0.07 us: columns_of(): column = jnp.concatenate(parts)]
    unnamed x231 -> x54, local copies, waits for them, and re-layouts: 32.3 us -> 5.84 us
  transfers between devices with their start and end apart: 4 -> 5, of which waited for: 3 -> 3; matrix products, arithmetic and copies ran while one was open for 9% -> 13% of each run, Pallas kernels for 0% -> 5%
where the time goes in v1:
time: 878 us; the launch traced here: 874 us
  waiting for transfers between devices  469 us (53%)
  Pallas kernels  135 us (15%)
  blocking collectives  84.4 us (10%)
  local copies, waits for them, and re-layouts  76.9 us (9%)
  other arithmetic  75.3 us (9%)
  between operations  26.9 us (3%)
    reduce_scatter x1, waiting for transfers between devices, per_device(): lax.psum_scatter(table_term, 'dp', scatter_dimension=0, tiled=True)  339 us
    unnamed x5, waiting for transfers between devices  105 us
    pallas_call x1, Pallas kernels, run_student(): pl.pallas_call(student_kernel, grid=(seqs,), out_shape=(jax.ShapeDtypeStr...  95 us
    psum x1, blocking collectives, per_device(): grad_norm = jnp.sqrt(lax.psum(squares, 'dp'))  46.9 us
    pallas_call x1, Pallas kernels, run_teacher(): pl.pallas_call(teacher_kernel, grid=(seqs,), out_shape=jax.ShapeDtypeStru...  39.9 us
    scatter-add x1, other arithmetic, per_device(): table_term = jnp.zeros((table_rows.shape[0], D), f32).at[index].add(updates)  39.6 us
    psum x1, blocking collectives, per_device(): global_count = lax.psum(jnp.sum(lengths).astype(f32), 'dp')  37.5 us
    all_gather x1, waiting for transfers between devices, per_device(): lax.all_gather(word_table.astype(bf16), 'dp', axis=0, tiled=True)  25.1 us
  transfers between devices with their start and end apart: 5, of which 3 were waited for; matrix products, arithmetic and copies ran while one was open for 13% of the time, Pallas kernels for 5%

profile of v1, /device:TPU:0, one launch (start us, length us, event | category | flops | bytes accessed | tf_op | source)
XLA Modules:
  0.0 874.2 jit_solution(2856563470918363581)
XLA Ops:
  7.2 1.0 convert_element_type.42
  8.3 0.7 reshape.343
  9.0 2.1 convert_element_type.39
  11.2 0.1 fusion.32
  11.3 6.4 collective-permute-start
  17.7 0.6 reduce_sum.63
  19.1 0.1 copy.41
  19.3 0.1 copy.40
  19.4 0.1 copy.39
  19.6 0.7 fusion.31
  20.3 0.8 maximum_bitcast_fusion.rest_0_
  21.1 0.5 iota_multiply_fusion.off_ref
  21.6 37.5 %psum.21 = f32[]{:T(128)} all-reduce(f32[]{:T(128)S(6)} %convert_element_type.38), channel_id=1, replica_groups=mesh['dp'=32] {'dp'}, use_global_device_ids=true, to_apply=%region_1.2 | all-reduce | flops 1 | bytes 8 | tf_op jit(solution)/shard_map/psum | solution.py:658
  59.1 1.7 slice.248.pos_in
  60.9 0.7 copy.42
  61.6 0.2 slice.262
  61.8 1.0 copy.44
  62.8 0.2 reshape.313
  63.1 1.0 copy.43
  65.5 20.7 %gather_fusion.1 = bf16[4096,256]{1,0:T(8,128)(2,1)S(1)} fusion(bf16[31034,256]{1,0:T(8,128)(2,1)} %param.16, s32[4096]{0:T(1024)S(1)} %broadcast_clamp_fusion), kind=kCustom, calls=%fused_computation.1 | custom fusion | bytes 4210688 | tf_op jit(solution)/shard_map/jit(_take)/gather | solution.py:665
  86.1 0.6 pad_add_fusion.2.len_ref
  86.7 0.6 compare_and_fusion
  87.3 1.7 broadcast_select_fusion.rows_ref
  89.0 3.3 broadcast_in_dim.50.col_ref
  92.3 39.9 %teacher.1.target_ref = f32[8,256,512]{2,1,0:T(8,128)} custom-call(s32[8]{0:T(128)} %pad_add_fusion.2.len_ref, s32[8]{0:T(128)} %iota_multiply_fusion.off_ref, bf16[4096,256]{1,0:T(8,128)(2,1)} %broadcast_select_fusion.rows_ref, bf16[512,256]{1,0:T(8,128)(2,1)} %slice.248.pos_in, f32[5120,128]{1,0:T(8,128)} %broadcast_in_dim.50.col_ref, ...), custom_call_target="tpu_custom_call" | custom-call | tf_op jit(solution)/shard_map/teacher/pallas_call | solution.py:475
  132.2 0.6 broadcast_clamp_fusion.1
  132.8 11.5 %reduce.1 = bf16[32,26880]{1,0:T(8,128)(2,1)S(1)} reduce(bf16[32,1,26880]{2,1,0:T(2,128)(2,1)} %all-gather.6.cloned.1.call-done, bf16[]{:T(256)} %constant.144), dimensions={1}, to_apply=%all-gather.reduce_sub_computation | reduce | bytes 3440642 | tf_op jit(solution)/shard_map/all_gather | solution.py:657
  144.3 3.0 reshape.344
  147.3 0.7 slice_reduce_fusion
  148.7 0.6 slice_reduce_fusion.2
  149.9 0.6 slice_reduce_fusion.1
  153.3 0.1 fusion.20
  153.3 0.1 broadcast_in_dim.51
  153.4 0.1 reshape.314
  153.5 0.9 fusion.27
  154.4 0.2 slice.285.rest_9_
  154.7 0.8 copy.46.rest_1_
  155.5 0.8 copy.49.rest_4_
  156.5 0.9 copy.45.rest_0_
  157.5 1.3 slice.283.rest_8_
  158.8 1.0 copy.47.rest_2_
  159.8 1.0 copy.48.rest_3_
  160.8 0.6 pad_bitcast_fusion
  161.5 0.6 copy-done.15
  162.1 25.1 %all-gather.4.cloned.1.call-done = bf16[31232,256]{1,0:T(8,128)(2,1)} async-done(((bf16[976,256]{1,0:T(8,128)(2,1)}), bf16[31232,256]{1,0:T(8,128)(2,1)}) %all-gather.4.cloned.1.call-update) | async-done | bytes 15990800 | tf_op jit(solution)/shard_map/all_gather | solution.py:656
  187.2 22.5 %gather_fusion = bf16[4096,256]{1,0:T(8,128)(2,1)S(1)} fusion(bf16[31232,256]{1,0:T(8,128)(2,1)} %all-gather.4.cloned.1.call-done, s32[4096]{0:T(1024)} %broadcast_clamp_fusion.1), kind=kCustom, calls=%fused_computation | custom fusion | bytes 4210688 | tf_op jit(solution)/shard_map/jit(_take)/gather | solution.py:681
  209.8 1.7 broadcast_select_fusion.1.rows_ref
  211.6 1.7 slice.294.pos_in
  213.3 3.2 broadcast_in_dim.52.col_ref
  216.5 95.0 %student.1 = (f32[6720,128]{1,0:T(8,128)}, bf16[8,256,512]{2,1,0:T(8,128)(2,1)}, f32[256,512]{1,0:T(8,128)}, f32[8,512]{1,0:T(8,128)}) custom-call(s32[8]{0:T(128)} %pad_add_fusion.2.len_ref, s32[8]{0:T(128)} %iota_multiply_fusion.off_ref, f32[1]{0:T(128)} %bitcast.3.fac_ref, bf16[4096,256]{1,0:T(8,128)(2,1)} %broadcast_select_fusion.1.rows_ref, ...), custom_call_target="tpu_custom_call" | custom-call | tf_op jit(solution)/shard_map/student/pallas_call | solution.py:489
  311.7 0.9 copy-done.10
  312.6 0.2 copy.51
  312.8 0.5 copy-done.4
  313.3 2.5 convert_bitcast_fusion
  315.8 5.3 copy.50
  321.2 39.6 %scatter_custom_fusion = f32[31232,256]{1,0:T(8,128)} fusion(s32[4608]{0:T(1024)S(1)} %fusion.7, f32[]{:T(128)} %constant.35.clone.1, f32[512,256]{1,0:T(8,128)S(1)} %copy.51, f32[]{:T(128)} %constant.145, f32[4096,256]{1,0:T(8,128)} %bitcast.36), kind=kCustom, calls=%fused_computation.3 | custom fusion | flops 2359296 | bytes 36700168 | tf_op jit(solution)/shard_map/scatter-add | solution.py:694
  361.6 0.6 reduce_sum.69
  362.2 105.3 %all-reduce.10.cloned.1.call-done = f32[860160]{0:T(1024)} async-done(((f32[860160]{0:T(1024)}), f32[860160]{0:T(1024)}) %all-reduce.10.cloned.1.call-update) | async-done | bytes 3440656
  467.5 1.6 multiply_reduce_fusion.1
  469.1 338.7 %reduce-scatter.2.cloned.1.call-done = f32[976,256]{1,0:T(8,128)} async-done(((f32[31232,256]{1,0:T(8,128)}), f32[976,256]{1,0:T(8,128)}) %reduce-scatter.2.cloned.1.call-update) | async-done | bytes 999440 | tf_op jit(solution)/shard_map/reduce_scatter | solution.py:695
  807.8 2.1 multiply_reduce_fusion
  811.2 46.9 %all-reduce.7 = (f32[]{:T(128)}, f32[]{:T(128)}) all-reduce(f32[]{:T(128)S(6)} %add.177, f32[]{:T(128)} %reduce_sum.69), channel_id=1, replica_groups=mesh['dp'=32] {'dp'}, use_global_device_ids=true, to_apply=%region_10.11 | all-reduce | flops 2 | bytes 16 | tf_op jit(solution)/shard_map/psum | solution.py:698
  860.2 1.8 multiply_subtract_fusion.1
  861.9 3.3 multiply_subtract_fusion
  (96 shorter events, 1.3 us)
Async XLA Ops:
  7.2 4.0 copy-start.21
  7.2 4.1 copy-start.18
  7.2 11.8 %copy-start.5 = (bf16[790016]{0:T(1024)(128)(2,1)S(1)}, bf16[790016]{0:T(1024)(128)(2,1)}, u32[]{:S(2)}) copy-start(bf16[790016]{0:T(1024)(128)(2,1)} %param.17) | copy-start | bytes 4740100
  7.2 125.6 %all-gather.6.cloned.1.call-start = ((), (), s32[]{:S(2)}) async-start(), calls=%async_computation.3 | async-start | bytes 3548160 | tf_op jit(solution)/shard_map/all_gather | solution.py:657
  9.0 10.6 %copy-start.22 = (f32[2]{0:T(128)S(1)}, f32[2]{0:T(128)}, u32[]{:S(2)}) copy-start(f32[2]{0:T(128)} %param.15) | copy-start | bytes 28
  9.0 178.2 %all-gather.4.cloned.1.call-start = ((), (), s32[]{:S(2)}) async-start(), calls=%async_computation.1 | async-start | bytes 16490496 | tf_op jit(solution)/shard_map/all_gather | solution.py:656
  11.1 456.4 %all-reduce.10.cloned.1.call-start = ((), (), s32[]{:S(2)}) async-start(), calls=%async_computation.4 | async-start | bytes 6881280
  11.3 54.0 %collective-permute-start = (s32[5,512]{1,0:T(8,128)S(1)}, s32[5,512]{1,0:T(8,128)S(1)}, u32[]{:S(2)}, u32[]{:S(2)}) collective-permute-start(s32[5,512]{1,0:T(8,128)S(1)} %pad_add_fusion), channel_id=1, source_target_pairs={{0,31},{1,30},{2,29},{3,28},{4,27},{5,26},{6,25},{7,24},{8,23},{9,... | collective-permute-start | bytes 30728 | tf_op jit(solution)/shard_map/ppermute | solution.py:651
  144.3 8.9 %copy-start.20 = (f32[1284]{0:T(1024)S(1)}, f32[1284]{0:T(1024)}, u32[]{:S(2)}) copy-start(f32[1284]{0:T(1024)} %param.14) | copy-start | bytes 15412
  154.5 5.2 copy-start
  154.7 4.1 copy-start.6
  154.7 5.0 copy-start.7
  156.5 4.3 copy-start.14
  156.5 53.3 %copy-start.3 = (bf16[256,768]{1,0:T(8,128)(2,1)}, bf16[256,768]{1,0:T(8,128)(2,1)S(1)}, u32[]{:S(2)}) copy-start(bf16[256,768]{1,0:T(8,128)(2,1)S(1)} %constant_dynamic-update-slice_fusion.rest_5_) | copy-start | bytes 1179652
  158.7 51.0 %copy-start.1 = (bf16[256,1024]{1,0:T(8,128)(2,1)}, bf16[256,1024]{1,0:T(8,128)(2,1)S(1)}, u32[]{:S(2)}) copy-start(bf16[256,1024]{1,0:T(8,128)(2,1)S(1)} %slice.283.rest_8_) | copy-start | bytes 1572868
  161.5 0.6 copy-start.15
  162.1 47.7 %copy-start.17 = (pred[4096]{0:T(1024)(128)(4,1)S(1)}, pred[4096]{0:T(1024)(128)(4,1)}, u32[]{:S(2)}) copy-start(pred[4096]{0:T(1024)(128)(4,1)} %get-tuple-element.41) | copy-start | bytes 12292
  209.8 3.5 copy-start.16
  311.5 1.0 copy-start.10
  311.5 1.8 copy-start.4
  311.6 496.3 %reduce-scatter.2.cloned.1.call-start = ((), (), s32[]{:S(2)}) async-start(), calls=%async_computation.2 | async-start | bytes 32980992 | tf_op jit(solution)/shard_map/reduce_scatter | solution.py:695
  360.7 0.8 copy-start.19
  360.7 499.4 %copy-start.11 = (f32[26880]{0:T(1024)S(1)}, f32[26880]{0:T(1024)}, u32[]{:S(2)}) copy-start(f32[26880]{0:T(1024)} %param.21) | copy-start | bytes 322564
  360.7 499.4 %copy-start.12 = (f32[26880]{0:T(1024)S(1)}, f32[26880]{0:T(1024)}, u32[]{:S(2)}) copy-start(f32[26880]{0:T(1024)} %param.22) | copy-start | bytes 322564
  360.7 499.4 %copy-start.13 = (f32[26880]{0:T(1024)S(1)}, f32[26880]{0:T(1024)}, u32[]{:S(2)}) copy-start(f32[26880]{0:T(1024)} %param.23) | copy-start | bytes 322564
  360.8 501.2 %copy-start.8 = (f32[976,256]{1,0:T(8,128)S(1)}, f32[976,256]{1,0:T(8,128)}, u32[]{:S(2)}) copy-start(f32[976,256]{1,0:T(8,128)} %param.19) | copy-start | bytes 2998276
  360.8 501.2 %copy-start.9 = (f32[976,256]{1,0:T(8,128)S(1)}, f32[976,256]{1,0:T(8,128)}, u32[]{:S(2)}) copy-start(f32[976,256]{1,0:T(8,128)} %param.20) | copy-start | bytes 2998276
  360.8 501.1 %copy-start.2 = (f32[976,256]{1,0:T(8,128)S(1)}, f32[976,256]{1,0:T(8,128)}, u32[]{:S(2)}) copy-start(f32[976,256]{1,0:T(8,128)} %param.18) | copy-start | bytes 2998276
Sparse Core Ops, SparseCore 0:
  11.4 62.5 all-gather.5
  76.8 110.3 all-gather.3
  311.7 155.7 all-reduce.9
  469.8 337.9 reduce-scatter.1

commit v2 on v1

--- a/solution.py
+++ b/solution.py
@@ -169,7 +169,7 @@
         sc["out"][:, c : c + width] = out
 
 
-def backward_body(span, length, factor, target_ref, col_ref, w, sc, acc, add_ref, loss_ref, grad_ref, pos_add):
+def backward_body(span, length, factor, target_ref, col_ref, w, sc, acc, add_ref, loss_ref, grad_ref, pos_add, eyes):
     def add(row, values):
         add_ref[row : row + values.shape[0], :] += lanes_in(values)
 
@@ -257,7 +257,9 @@
         add(D, d_norm)
         d_embedded = standardise_back(d_norm * gain, hat, sc["scale"][0:1, cols])
         pos_add[:, cols] += d_embedded
-        grad_ref[0, :, cols] = d_embedded.astype(bf16)
+        d_low = d_embedded.astype(bf16)
+        grad_ref[0, :, cols] = d_low
+        sc["grad_rows"][cols, :] = nt(eyes[width], d_low)
     if span < LEN:
         grad_ref[0, :, span:LEN] = jnp.zeros((D, LEN - span), bf16)
 
@@ -323,6 +325,7 @@
     ("d_context", (D, LEN), bf16),
     ("delta", (8, LEN), f32),
     ("d_qkv", (3 * D, LEN), bf16),
+    ("grad_rows", (LEN, D), f32),
 )
 ACCS = (
     ("qkv", (D, 3 * D)),
@@ -361,21 +364,21 @@
     by_span(length, body)
 
 
-def student_kernel(len_ref, off_ref, fac_ref, rows_ref, pos_in, target_ref, col_ref, slope_in, lag_in, *rest):
+def student_kernel(flat_len, len_ref, off_ref, slot_ref, fac_ref, rows_ref, pos_in, target_ref, col_ref, slope_in, lag_in, *rest):
     w = {name: rest[i] for i, (name, _) in enumerate(STUDENT_W)}
     rest = rest[len(STUDENT_W) :]
-    flat_ref, grad_ref, pos_add, loss_ref = rest[:4]
+    flat_ref, grad_ref, packed_ref, loss_ref = rest[:4]
     scratch = rest[4:]
     sc = {entry[0]: scratch[i] for i, entry in enumerate(STUDENT_S)}
     scratch = scratch[len(STUDENT_S) :]
     acc = {entry[0]: scratch[i] for i, entry in enumerate(ACCS)}
-    add_ref, pos_ref, eye_one, eye_two = scratch[len(ACCS) :]
+    add_ref, pos_add, slots_f32, pos_ref, eye_one, eye_two = scratch[len(ACCS) :]
     s = pl.program_id(0)
 
     @pl.when(s == 0)
     def _():
         set_up(pos_in, pos_ref, {128: eye_one, 256: eye_two})
-        for ref in list(acc.values()) + [add_ref, pos_add, loss_ref]:
+        for ref in list(acc.values()) + [add_ref, pos_add, loss_ref, slots_f32]:
             ref[...] = jnp.zeros(ref.shape, f32)
 
     eyes = {128: eye_one, 256: eye_two}
@@ -390,10 +393,19 @@
         offset = pl.multiple_of(off_ref[s], 16)
         forward_body(span, offset, length, True, rows_ref, pos_ref, col_ref, w, sc, Read())
         backward_body(
-            span, length, fac_ref[0], target_ref, col_ref, w, sc, acc, add_ref, loss_ref, grad_ref, pos_add
+            span, length, fac_ref[0], target_ref, col_ref, w, sc, acc, add_ref, loss_ref, grad_ref, pos_add, Read()
         )
 
     by_span(length, body)
+
+    def place(step, carry):
+        for u in range(8):
+            at = step * 8 + u
+            slot = slot_ref[s, at]
+            slots_f32[pl.ds(slot, 1), :] = sc["grad_rows"][pl.ds(at, 1), :]
+        return carry
+
+    lax.fori_loop(0, (length + 7) // 8, place, 0)
 
     @pl.when(s == pl.num_programs(0) - 1)
     def _():
@@ -447,7 +459,12 @@
             flat_ref[R_LOGIT + j : R_LOGIT + j + 1, :] = (
                 piece[0:1] * slope_in[j : j + 1, :] + lag_in[j : j + 1, :]
             )
-        flat_ref[R_USED:, :] = jnp.zeros((flat_ref.shape[0] - R_USED, LANES), f32)
+        flat_ref[R_USED:flat_len, :] = jnp.zeros((flat_len - R_USED, LANES), f32)
+        for j in range(2):
+            flat_ref[pl.ds(flat_len + j, LEN, stride=2), :] = jnp.transpose(
+                pos_add[j * LANES : (j + 1) * LANES, :]
+            )
+        packed_ref[...] = slots_f32[0 : packed_ref.shape[0], :].astype(bf16)
 
 
 def whole_spec():
@@ -484,36 +501,43 @@
     )(lengths, offsets, rows, places, columns, *[weights[name] for name, _ in TEACHER_W])
 
 
-def run_student(lengths, offsets, factor, rows, places, target, columns, slopes, lag, weights, flat_rows):
+def run_student(
+    lengths, offsets, slots, factor, rows, places, target, columns, slopes, lag, weights, flat_len, slot_rows
+):
     seqs = lengths.shape[0]
     return pl.pallas_call(
-        student_kernel,
+        functools.partial(student_kernel, flat_len),
         grid=(seqs,),
         out_shape=(
-            jax.ShapeDtypeStruct((flat_rows, LANES), f32),
+            jax.ShapeDtypeStruct((flat_len + 2 * LEN, LANES), f32),
             jax.ShapeDtypeStruct((seqs, D, LEN), bf16),
-            jax.ShapeDtypeStruct((D, LEN), f32),
+            jax.ShapeDtypeStruct((slot_rows, D), bf16),
             jax.ShapeDtypeStruct((8, LEN), f32),
         ),
-        in_specs=[smem_spec()] * 3
+        in_specs=[smem_spec()] * 4
         + [whole_spec()] * 2
         + [seq_spec()]
         + [whole_spec()] * (3 + len(STUDENT_W)),
         out_specs=(
-            pl.BlockSpec((flat_rows, LANES), lambda s: (0, 0)),
+            pl.BlockSpec((flat_len + 2 * LEN, LANES), lambda s: (0, 0)),
             seq_spec(),
-            pl.BlockSpec((D, LEN), lambda s: (0, 0)),
+            pl.BlockSpec((slot_rows, D), lambda s: (0, 0)),
             pl.BlockSpec((8, LEN), lambda s: (0, 0)),
         ),
         scratch_shapes=[pltpu.VMEM(shape, kind) for _, shape, kind in STUDENT_S]
         + [pltpu.VMEM(shape, f32) for _, shape in ACCS]
-        + [pltpu.VMEM((A_ROWS, LANES), f32)]
+        + [
+            pltpu.VMEM((A_ROWS, LANES), f32),
+            pltpu.VMEM((D, LEN), f32),
+            pltpu.VMEM((slot_rows + 8, D), f32),
+        ]
         + extra_scratch(),
         compiler_params=pltpu.CompilerParams(vmem_limit_bytes=VMEM_LIMIT),
         name="student",
     )(
         lengths,
         offsets,
+        slots,
         factor,
         rows,
         places,
@@ -523,6 +547,372 @@
         lag,
         *[weights[name] for name, _ in STUDENT_W],
     )
+
+
+MESH = pl.DeviceIdType.MESH
+
+
+def room(n):
+    return min(LANES, max(32, 8 * LEN // n))
+
+
+def greet_all(me, n):
+    barrier = pltpu.get_barrier_semaphore()
+
+    def signal(k, carry):
+        pl.semaphore_signal(barrier, inc=1, device_id=(me ^ k,), device_id_type=MESH)
+        return carry
+
+    lax.fori_loop(1, n, signal, 0)
+    pl.semaphore_wait(barrier, n - 1)
+
+
+def copy_to(source, target, send, receive, device):
+    return pltpu.make_async_remote_copy(
+        src_ref=source,
+        dst_ref=target,
+        send_sem=send,
+        recv_sem=receive,
+        device_id=(device,),
+        device_id_type=MESH,
+    )
+
+
+def route_kernel(n, owner_ref, local_ref, stat_ref, slot_ref, got_ref, tile_ref, send_sem, recv_sem):
+    me = lax.axis_index("dp")
+    cap = room(n)
+    seqs = owner_ref.shape[0]
+    upper = (
+        lax.broadcasted_iota(jnp.int32, (256, 256), 0)
+        <= lax.broadcasted_iota(jnp.int32, (256, 256), 1)
+    ).astype(bf16)
+    base = jnp.zeros((n, 1), f32)
+    listed = jnp.zeros((n, LANES), f32)
+    for s in range(seqs):
+        for c in range(0, LEN, 256):
+            owner = owner_ref[s : s + 1, c : c + 256]
+            mine = (lax.broadcasted_iota(jnp.int32, (n, 256), 0) == owner).astype(f32)
+            before = nn(mine.astype(bf16), upper)
+            rank = jnp.sum(mine * (before - 1.0 + base), axis=0, keepdims=True).astype(jnp.int32)
+            fits = (owner >= 0) & (rank < cap)
+            slot_ref[s : s + 1, c : c + 256] = jnp.where(fits, owner * cap + rank, n * cap)
+            place = (
+                lax.broadcasted_iota(jnp.int32, (LANES, 256), 0) == jnp.where(fits, rank, -1)
+            ).astype(f32)
+            listed = listed + lax.dot_general(
+                mine * local_ref[s : s + 1, c : c + 256],
+                place,
+                (((1,), (1,)), ((), ())),
+                preferred_element_type=f32,
+                precision=lax.Precision.HIGHEST,
+            )
+            base = base + before[:, 255:256]
+    over = jnp.max(base, axis=0, keepdims=True) > cap
+    lane = lax.broadcasted_iota(jnp.int32, (n, LANES), 1)
+    tile_ref[...] = jnp.zeros(tile_ref.shape, jnp.int32)
+    tile_ref[pl.ds(0, n, stride=8), :] = (listed + 0.5).astype(jnp.int32) - 1
+    tile_ref[pl.ds(1, n, stride=8), :] = jnp.where(
+        lane == 0, stat_ref[0], jnp.where(lane == 1, over.astype(jnp.int32), 0)
+    )
+    greet_all(me, n)
+
+    def tile(ref, i):
+        return ref.at[pl.ds(pl.multiple_of(i * 8, 8), 8), :]
+
+    def copy(k):
+        return copy_to(
+            tile(tile_ref, me ^ k), tile(got_ref, me), send_sem.at[k], recv_sem.at[k], me ^ k
+        )
+
+    def start(k, carry):
+        copy(k).start()
+        return carry
+
+    def finish(k, carry):
+        copy(k).wait()
+        return carry
+
+    lax.fori_loop(1, n, start, 0)
+    own = pl.ds(pl.multiple_of(me * 8, 8), 8)
+    got_ref[own, :] = tile_ref[own, :]
+    lax.fori_loop(1, n, finish, 0)
+
+
+def run_route(n, owner, local, stat):
+    return pl.pallas_call(
+        functools.partial(route_kernel, n),
+        out_shape=(
+            jax.ShapeDtypeStruct(owner.shape, jnp.int32),
+            jax.ShapeDtypeStruct((8 * n, LANES), jnp.int32),
+        ),
+        in_specs=[whole_spec(), whole_spec(), smem_spec()],
+        out_specs=(whole_spec(), whole_spec()),
+        scratch_shapes=[
+            pltpu.VMEM((8 * n, LANES), jnp.int32),
+            pltpu.SemaphoreType.DMA((n,)),
+            pltpu.SemaphoreType.DMA((n,)),
+        ],
+        compiler_params=pltpu.CompilerParams(
+            collective_id=1, has_side_effects=True, vmem_limit_bytes=VMEM_LIMIT
+        ),
+        name="route",
+    )(owner, local, stat)
+
+
+def plan(n, flat_len):
+    chips = n // 2
+    plane = 2 ** ((chips.bit_length() - 1) // 2)
+    flat_seg = flat_len // n
+    flat_pad = -(-flat_seg // 16) * 16
+    place_seg = 2 * LEN // n
+    return plane, chips // plane, flat_seg, flat_pad, place_seg, flat_pad + -(-place_seg // 16) * 16
+
+
+def place_tile(n):
+    return max(8, 2 * LEN // n)
+
+
+def exchange_kernel(n, flat_len, sparse, *refs):
+    plane, planes, flat_seg, flat_pad, place_seg, seg = plan(n, flat_len)
+    chips = n // 2
+    cap = room(n)
+    tile = place_tile(n)
+    flat_ref, loss_ref = refs[:2]
+    refs = refs[2:]
+    if sparse:
+        packed_ref, list_ref = refs[:2]
+        refs = refs[2:]
+    else:
+        given_ref = refs[0]
+        refs = refs[1:]
+    table_ref, sums_ref, stat_out = refs[:3]
+    (stage, one_in, two_out, two_in, total, three_out, three_in, place_in, stat_in) = refs[3:12]
+    refs = refs[12:]
+    if sparse:
+        rows_in = refs[0]
+        refs = refs[1:]
+    one_sem, two_sem, three_sem, place_sem, stat_sem, row_sem = refs
+    me = lax.axis_index("dp")
+    core = lax.rem(me, 2)
+    chip = me // 2
+    mid = lax.rem(chip, plane)
+    high = chip // plane
+    vrows = table_ref.shape[0]
+
+    greet_all(me, n)
+    pad = jnp.zeros((16, LANES), f32)
+    for o in range(n):
+        spot = stage.at[o % 2, o // 2]
+        if flat_pad > flat_seg:
+            spot[flat_pad - 16 : flat_pad, :] = pad
+        if seg > flat_pad + place_seg:
+            spot[seg - 16 : seg, :] = pad
+        spot[0:flat_seg, :] = flat_ref[o * flat_seg : (o + 1) * flat_seg, :]
+        at = flat_len + o * place_seg
+        spot[flat_pad : flat_pad + place_seg, :] = flat_ref[at : at + place_seg, :]
+    first = copy_to(stage.at[1 - core], one_in, one_sem.at[0], one_sem.at[1], me ^ 1)
+    first.start()
+
+    if sparse:
+
+        def bucket(ref, i):
+            return ref.at[pl.ds(pl.multiple_of(i * cap, cap), cap), :]
+
+        def row_copy(k):
+            return copy_to(
+                bucket(packed_ref, me ^ k), bucket(rows_in, me), row_sem.at[0, k], row_sem.at[1, k], me ^ k
+            )
+
+        def start_row(i, carry):
+            row_copy(n - i).start()
+            return carry
+
+        lax.fori_loop(1, n, start_row, 0)
+        own = pl.ds(pl.multiple_of(me * cap, cap), cap)
+        rows_in[own, :] = packed_ref[own, :]
+
+    first.wait()
+    for m in range(plane):
+        for h in range(planes):
+            c = h * plane + m
+            two_out[m, h] = (stage[core, c] + one_in[c]).astype(bf16)
+    second = []
+    for k in range(1, plane):
+        m = lax.rem(mid + k, plane)
+        second.append(
+            copy_to(
+                two_out.at[m],
+                two_in.at[k - 1],
+                two_sem.at[0, k],
+                two_sem.at[1, k],
+                (high * plane + m) * 2 + core,
+            )
+        )
+        second[-1].start()
+    for copy in second:
+        copy.wait()
+    for h in range(planes):
+        c = h * plane + mid
+        value = stage[core, c] + one_in[c]
+        for k in range(1, plane):
+            value = value + two_in[k - 1, h].astype(f32)
+        total[h] = value
+        three_out[h] = value.astype(bf16)
+    third = []
+    for k in range(1, planes):
+        h = lax.rem(high + k, planes)
+        third.append(
+            copy_to(
+                three_out.at[h],
+                three_in.at[k - 1],
+                three_sem.at[0, k],
+                three_sem.at[1, k],
+                (h * plane + mid) * 2 + core,
+            )
+        )
+        third[-1].start()
+    for copy in third:
+        copy.wait()
+    value = total[high]
+    for k in range(1, planes):
+        value = value + three_in[k - 1].astype(f32)
+    total[0] = value
+    sums_ref[...] = value[:flat_pad]
+
+    owners = range(VOCAB // vrows, (VOCAB + LEN - 1) // vrows + 1)
+    place_out = total.at[0, pl.ds(flat_pad, tile), :]
+    place_spot = pl.ds(pl.multiple_of(me * tile, 8), tile)
+    for i, o in enumerate(owners):
+        place_copy = copy_to(
+            place_out, place_in.at[place_spot, :], place_sem.at[0, i], place_sem.at[1, me], o
+        )
+        pl.when(me != o)(place_copy.start)
+
+    squares = jnp.sum(jnp.sum(value * value, axis=0, keepdims=True), axis=1, keepdims=True)
+    if sparse:
+        def add_pair(i, carry):
+            pl.when(i > 0)(lambda: row_copy(2 * i).wait_recv())
+            row_copy(2 * i + 1).wait_recv()
+            a = chip ^ i
+            lists = jnp.concatenate(
+                [
+                    list_ref[pl.ds(pl.multiple_of(a * 16 + 8 * j, 8), 8), :][0:1, :cap]
+                    for j in range(2)
+                ],
+                axis=1,
+            )
+            pick = (lax.broadcasted_iota(jnp.int32, (vrows, 2 * cap), 0) == lists).astype(bf16)
+            both = rows_in[pl.ds(pl.multiple_of(a * 2 * cap, 2 * cap), 2 * cap), :]
+            table_ref[...] += nn(pick, both)
+            return carry
+
+        table_ref[...] = jnp.zeros(table_ref.shape, f32)
+        lax.fori_loop(0, chips, add_pair, 0)
+    else:
+        table_ref[...] = given_ref[...]
+    grads = table_ref[...]
+    squares = squares + jnp.sum(
+        jnp.sum(grads * grads, axis=0, keepdims=True), axis=1, keepdims=True
+    )
+    loss = jnp.sum(jnp.sum(loss_ref[...], axis=0, keepdims=True), axis=1, keepdims=True)
+    lane = lax.broadcasted_iota(jnp.int32, (8, LANES), 1)
+    stat_out[...] = jnp.where(lane == 0, squares, jnp.where(lane == 1, loss, 0.0))
+
+    def stat_copy(k):
+        return copy_to(
+            stat_out, stat_in.at[me], stat_sem.at[0, k], stat_sem.at[1, k], me ^ k
+        )
+
+    def start_stat(k, carry):
+        stat_copy(k).start()
+        return carry
+
+    def finish_stat(k, carry):
+        stat_copy(k).wait()
+        return carry
+
+    lax.fori_loop(1, n, start_stat, 0)
+    stat_in[me] = stat_out[...]
+
+    for i, o in enumerate(owners):
+
+        @pl.when(me == o)
+        def _():
+            place_in[place_spot, :] = place_out[...]
+
+            def wait_place(j, carry):
+                copy_to(
+                    place_out,
+                    place_in.at[pl.ds(pl.multiple_of(j * tile, 8), tile), :],
+                    place_sem.at[0, i],
+                    place_sem.at[1, j],
+                    me ^ 1,
+                ).wait_recv()
+                return carry
+
+            lax.fori_loop(0, o, wait_place, 0)
+            lax.fori_loop(o + 1, n, wait_place, 0)
+            low = max(0, o * vrows - VOCAB)
+            top = min(LEN, (o + 1) * vrows - VOCAB)
+            at = VOCAB + low - o * vrows
+            if tile > place_seg:
+                for d in range(n):
+                    place_in[d * place_seg : (d + 1) * place_seg, :] = place_in[
+                        d * tile : d * tile + place_seg, :
+                    ]
+            for j in range(2):
+                table_ref[at : at + top - low, j * LANES : (j + 1) * LANES] += place_in[
+                    pl.ds(2 * low + j, top - low, stride=2), :
+                ]
+
+    lax.fori_loop(1, n, finish_stat, 0)
+    stat_out[...] = jnp.sum(stat_in[...], axis=0)
+    for i, o in enumerate(owners):
+        place_copy = copy_to(
+            place_out, place_in.at[place_spot, :], place_sem.at[0, i], place_sem.at[1, me], o
+        )
+        pl.when(me != o)(place_copy.wait_send)
+    if sparse:
+
+        def finish_row(k, carry):
+            row_copy(k).wait_send()
+            return carry
+
+        lax.fori_loop(1, n, finish_row, 0)
+
+
+def run_exchange(n, vrows, flat_grads, loss_rows, sparse, given):
+    flat_len = flat_grads.shape[0] - 2 * LEN
+    plane, planes, flat_seg, flat_pad, place_seg, seg = plan(n, flat_len)
+    count = len(range(VOCAB // vrows, (VOCAB + LEN - 1) // vrows + 1))
+    dma = pltpu.SemaphoreType.DMA
+    return pl.pallas_call(
+        functools.partial(exchange_kernel, n, flat_len, sparse),
+        out_shape=(
+            jax.ShapeDtypeStruct((vrows, D), f32),
+            jax.ShapeDtypeStruct((flat_pad, LANES), f32),
+            jax.ShapeDtypeStruct((8, LANES), f32),
+        ),
+        in_specs=[whole_spec()] * (2 + len(given)),
+        out_specs=(whole_spec(),) * 3,
+        scratch_shapes=[
+            pltpu.VMEM((2, n // 2, seg, LANES), f32),
+            pltpu.VMEM((n // 2, seg, LANES), f32),
+            pltpu.VMEM((plane, planes, seg, LANES), bf16),
+            pltpu.VMEM((plane - 1, planes, seg, LANES), bf16),
+            pltpu.VMEM((planes, seg, LANES), f32),
+            pltpu.VMEM((planes, seg, LANES), bf16),
+            pltpu.VMEM((planes - 1, seg, LANES), bf16),
+            pltpu.VMEM((n * place_tile(n), LANES), f32),
+            pltpu.VMEM((n, 8, LANES), f32),
+        ]
+        + ([pltpu.VMEM((n * room(n), D), bf16)] if sparse else [])
+        + [dma((2,)), dma((2, plane)), dma((2, planes)), dma((2, max(n, count))), dma((2, n)), dma((2, n))],
+        compiler_params=pltpu.CompilerParams(
+            collective_id=2 if sparse else 3, has_side_effects=True, vmem_limit_bytes=VMEM_LIMIT
+        ),
+        name="exchange" if sparse else "exchange_dense",
+    )(flat_grads, loss_rows, *given)
 
 
 clip_norm = 0.002
@@ -625,6 +1015,10 @@
 
 def pad_rows(values):
     return jnp.pad(values, (0, 16 * LANES - values.shape[0])).reshape(16, LANES)
+
+
+def rows_of(table, ids):
+    return table.at[ids.reshape(-1)].get(mode="promise_in_bounds")
 
 
 def per_device(
@@ -644,6 +1038,21 @@
 ):
     seqs = token_ids.shape[0]
     half = seqs // 2
+    vrows = word_table.shape[0]
+    flat_len = layer_flat.shape[0] * devices // LANES
+    own = layer_flat.shape[0]
+    own_rows = -(-own // D)
+    pad = -(vrows + own_rows) % 16
+    block = vrows + own_rows + pad
+    shard = jnp.concatenate(
+        [
+            word_table.astype(bf16),
+            jnp.pad(layer_flat.astype(bf16), (0, own_rows * D - own)).reshape(own_rows, D),
+            jnp.zeros((pad, D), bf16),
+        ]
+    )
+    gathered = lax.all_gather(shard, "dp", axis=0, tiled=True)
+
     mates = [(i, devices - 1 - i) for i in range(devices)]
     sent = jnp.concatenate(
         [token_ids[half:], jnp.pad(lengths[half:], (0, LEN - half)).reshape(1, LEN)]
@@ -653,51 +1062,71 @@
     lens = jnp.concatenate([lengths[:half], got[half, :half]])
     offsets = jnp.arange(seqs, dtype=jnp.int32) * LEN
 
-    table_rows = lax.all_gather(word_table.astype(bf16), "dp", axis=0, tiled=True)
-    flat_rows = lax.all_gather(layer_flat.astype(bf16), "dp", axis=0, tiled=True)
-    global_count = lax.psum(jnp.sum(lengths).astype(f32), "dp")
+    owner = ids // vrows
+    valid = jnp.arange(LEN)[None, :] < lens[:, None]
+    slots, listed = run_route(
+        devices,
+        jnp.where(valid, owner, -1),
+        (ids - owner * vrows + 1).astype(f32),
+        jnp.sum(lens).reshape(1),
+    )
+    stats = listed.reshape(devices, 8, LANES)[:, 1, :2]
+    global_count = jnp.sum(stats[:, 0]).astype(f32)
+    crowded = jnp.max(stats[:, 1]) > 0
     factor = ((2.0 / D) / global_count).reshape(1)
 
     teacher = unpack(teacher_flat, False)
     target = run_teacher(
         lens,
         offsets,
-        jnp.take(teacher_table, ids.reshape(-1), axis=0),
+        rows_of(teacher_table, ids),
         teacher_table[VOCAB : VOCAB + LEN],
         columns_of(teacher),
         kernel_weights(teacher, False),
     )
 
-    pieces = unpack(flat_rows, True)
+    blocks = gathered.reshape(devices, block, D)
+    flat_low = blocks[:, vrows : vrows + own_rows].reshape(devices, -1)[:, :own].reshape(-1)
+    pieces = unpack(flat_low, True)
     logits = pieces["gate_logits"].astype(f32)
     gates, gate_back = jax.vjp(lambda x: gate_values(x, gate_noise), logits)
     slopes = gate_back(jnp.ones_like(gates))[0]
     lag_value, lag_back = jax.vjp(lambda x: lagrangian(x, lagrange), logits)
     lag_weight = jnp.where(lax.axis_index("dp") == 0, 1.0, 0.0).astype(f32)
-    flat_term, grad_rows, place_grad, loss_rows = run_student(
+    places = []
+    for o in range(VOCAB // vrows, (VOCAB + LEN - 1) // vrows + 1):
+        low, top = max(VOCAB, o * vrows), min(VOCAB + LEN, (o + 1) * vrows)
+        places.append(gathered[o * (block - vrows) + low : o * (block - vrows) + top])
+    flat_grads, grad_rows, packed, loss_rows = run_student(
         lens,
         offsets,
+        slots,
         factor,
-        jnp.take(table_rows, ids.reshape(-1), axis=0),
-        table_rows[VOCAB : VOCAB + LEN],
+        rows_of(gathered, ids + owner * (block - vrows)),
+        jnp.concatenate(places) if len(places) > 1 else places[0],
         target,
         columns_of(pieces, gates),
         pad_rows(slopes),
         pad_rows(lag_back(lag_weight)[0]),
         kernel_weights(pieces, True),
-        flat_rows.shape[0] // LANES,
-    )
-    global_sum = lax.psum(jnp.sum(loss_rows), "dp")
-    updates = jnp.transpose(grad_rows, (0, 2, 1)).reshape(seqs * LEN, D).astype(f32)
-    index = jnp.concatenate([ids.reshape(-1), VOCAB + jnp.arange(LEN, dtype=jnp.int32)])
-    updates = jnp.concatenate([updates, place_grad.T])
-    table_term = jnp.zeros((table_rows.shape[0], D), f32).at[index].add(updates)
-    table_grad = lax.psum_scatter(table_term, "dp", scatter_dimension=0, tiled=True)
-    flat_grad = lax.psum_scatter(flat_term.reshape(-1), "dp", scatter_dimension=0, tiled=True)
-    squares = jnp.sum(table_grad * table_grad) + jnp.sum(flat_grad * flat_grad)
-    grad_norm = jnp.sqrt(lax.psum(squares, "dp"))
+        flat_len,
+        devices * room(devices),
+    )
+
+    def from_slots(_):
+        return run_exchange(devices, vrows, flat_grads, loss_rows, True, (packed, listed))
+
+    def from_rows(_):
+        updates = jnp.transpose(grad_rows, (0, 2, 1)).reshape(seqs * LEN, D).astype(f32)
+        table = jnp.zeros((devices * vrows, D), f32).at[ids.reshape(-1)].add(updates)
+        table = lax.psum_scatter(table, "dp", scatter_dimension=0, tiled=True)
+        return run_exchange(devices, vrows, flat_grads, loss_rows, False, (table,))
+
+    table_grad, sums, totals = lax.cond(crowded, from_rows, from_slots, 0)
+    flat_grad = sums[: own // LANES].reshape(-1)
+    grad_norm = jnp.sqrt(totals[0, 0])
     clip = jnp.minimum(1.0, clip_norm / (grad_norm + 1e-06))
-    total_loss = global_sum / global_count + lag_value
+    total_loss = totals[0, 1] / global_count + lag_value
     table_new = adam_step(word_table, table_first, table_second, table_grad * clip)
     flat_new = adam_step(layer_flat, flat_first, flat_second, flat_grad * clip)
     return (*table_new, *flat_new, total_loss, grad_norm)

time: 878 us -> 431 us (0.49)
  waiting for transfers between devices: 469 us -> 17.4 us
  Pallas kernels: 135 us -> 271 us
  blocking collectives: 84.4 us -> 0 us
  other arithmetic: 75.3 us -> 16.6 us
    reduce_scatter x1 -> x0, waiting for transfers between devices: 339 us -> none  [per_device(): lax.psum_scatter(table_term, 'dp', scatter_dimension=0, tiled=True)]
    pallas_call x1 -> x3, Pallas kernels: 95 us -> 230 us  [the longest x1 132 us: run_student(): pl.pallas_call(functools.partial(student_kernel, flat_len), grid=(seqs,),...]
    unnamed x5 -> x1, waiting for transfers between devices: 105 us -> 0.02 us
    psum x2 -> x0, blocking collectives: 84.4 us -> none  [the longest x1 46.9 us: per_device(): grad_norm = jnp.sqrt(lax.psum(squares, 'dp'))]
    scatter-add x1 -> x0, other arithmetic: 39.6 us -> none  [per_device(): table_term = jnp.zeros((table_rows.shape[0], D), f32).at[index].add(updates)]
    all_gather x1 -> x0, other arithmetic: 11.5 us -> none  [per_device(): lax.all_gather(layer_flat.astype(bf16), 'dp', axis=0, tiled=True)]
    all_gather x2 -> x1, waiting for transfers between devices: 25.1 us -> 17.4 us  [per_device(): gathered = lax.all_gather(shard, 'dp', axis=0, tiled=True)]
  transfers between devices with their start and end apart: 5 -> 2, of which waited for: 3 -> 1; matrix products, arithmetic and copies ran while one was open for 13% -> 9% of each run, Pallas kernels for 5% -> 14%
where the time goes in v2:
time: 431 us; the launch traced here: 423 us
  Pallas kernels  271 us (63%)
  local copies, waits for them, and re-layouts  83.4 us (19%)
  between operations  24.9 us (6%)
  waiting for transfers between devices  17.4 us (4%)
  other arithmetic  16.6 us (4%)
  starting transfers between devices  6.48 us (2%)
    pallas_call x1, Pallas kernels, run_student(): pl.pallas_call(functools.partial(student_kernel, flat_len), grid=(seqs,),...  132 us
    pallas_call x1, Pallas kernels, run_exchange(): pl.pallas_call(functools.partial(exchange_kernel, n, flat_len, sparse), o...  82.5 us
    gather x2, local copies, waits for them, and re-layouts, rows_of(): return table.at[ids.reshape(-1)].get(mode='promise_in_bounds')  47.9 us
    pallas_call x1, Pallas kernels, run_teacher(): pl.pallas_call(teacher_kernel, grid=(seqs,), out_shape=jax.ShapeDtypeStru...  41.5 us
    all_gather x1, waiting for transfers between devices, per_device(): gathered = lax.all_gather(shard, 'dp', axis=0, tiled=True)  17.4 us
    pallas_call x1, Pallas kernels, run_route(): pl.pallas_call(functools.partial(route_kernel, n), out_shape=(jax.ShapeDt...  15.7 us
    slice x17, local copies, waits for them, and re-layouts, unpack(): flat_vector[offset:offset + length].reshape(entry_shape)  9.13 us
  transfers between devices with their start and end apart: 2, of which 1 were waited for; matrix products, arithmetic and copies ran while one was open for 9% of the time, Pallas kernels for 14%

profile of v2, /device:TPU:0, one launch (start us, length us, event | category | flops | bytes accessed | tf_op | source)
XLA Modules:
  0.0 423.4 jit_solution(5305458320395616469)
XLA Ops:
  7.2 1.0 convert_element_type.45
  8.3 1.3 convert_element_type.44
  9.6 3.4 concatenate.32
  13.0 0.6 slice_reduce_fusion.6
  13.6 6.4 %collective-permute-start = (s32[5,512]{1,0:T(8,128)S(1)}, s32[5,512]{1,0:T(8,128)S(1)}, u32[]{:S(2)}, u32[]{:S(2)}) collective-permute-start(s32[5,512]{1,0:T(8,128)S(1)} %pad_add_fusion), channel_id=1, source_target_pairs={{0,31},{1,30},{2,29},{3,28},{4,27},{5,26},{6,25},{7,24},{8,23},{9,... | collective-permute-start | bytes 30728 | tf_op jit(solution)/shard_map/ppermute | solution.py:1060
  20.2 0.1 copy.30
  20.3 0.1 copy.29
  20.5 0.1 copy.28
  20.6 0.7 fusion.34
  21.3 0.8 maximum_bitcast_fusion.rest_0_
  22.1 0.1 fusion.31
  22.2 0.5 iota_multiply_fusion.off_ref
  22.7 1.7 slice.217.pos_in
  24.5 0.8 copy.31
  25.3 0.2 slice.231
  25.4 1.0 copy.33
  26.5 0.2 reshape.276
  26.7 1.0 copy.32
  28.4 0.6 slice_reduce_fusion.5
  29.0 0.1 pad_add_fusion.2.len_ref
  29.1 0.7 pad_add_fusion.1
  31.1 15.7 %route.1 = (s32[8,512]{1,0:T(8,128)}, s32[256,128]{1,0:T(8,128)S(1)}) custom-call(s32[8,512]{1,0:T(8,128)} %get-tuple-element.156.owner_ref, f32[8,512]{1,0:T(8,128)} %get-tuple-element.157.local_ref, s32[1]{0:T(128)} %bitcast.8.stat_ref), custom_call_target="tpu_custom_call" | custom-call | tf_op jit(solution)/shard_map/route/pallas_call | solution.py:642
  46.9 0.6 copy-done.4
  47.5 0.1 copy.40
  47.6 0.6 slice_reduce_fusion.3
  49.5 0.1 compare_select_fusion.1
  49.7 23.6 %gather_fusion.1 = bf16[4096,256]{1,0:T(8,128)(2,1)} fusion(bf16[31034,256]{1,0:T(8,128)(2,1)} %param.18, s32[4096]{0:T(1024)S(1)} %broadcast_clamp_fusion), kind=kCustom, calls=%fused_computation.1 | custom fusion | bytes 4210688 | tf_op jit(solution)/shard_map/gather | solution.py:1021
  73.3 3.2 broadcast_in_dim.17.col_ref
  76.5 41.5 %teacher.1.target_ref = f32[8,256,512]{2,1,0:T(8,128)} custom-call(s32[8]{0:T(128)} %copy-done.12, s32[8]{0:T(128)} %iota_multiply_fusion.off_ref, bf16[4096,256]{1,0:T(8,128)(2,1)} %gather_fusion.1, bf16[512,256]{1,0:T(8,128)(2,1)} %slice.217.pos_in, f32[5120,128]{1,0:T(8,128)} %broadcast_in_dim.17.col_ref, bf16[768,256]{1,0:T(8,128)(2,1)} %maximum_bitcast_fusion.rest_0_, ...), custom_call_target="tpu_custom_call" | custom-call | tf_op jit(solution)/shard_map/teacher/pallas_call | solution.py:492
  118.0 0.6 broadcast_clamp_fusion.1
  118.6 17.4 %all-gather.2.cloned.1.call-done = bf16[34816,256]{1,0:T(8,128)(2,1)} async-done(((bf16[1088,256]{1,0:T(8,128)(2,1)}), bf16[34816,256]{1,0:T(8,128)(2,1)}) %all-gather.2.cloned.1.call-update) | async-done | bytes 17825808 | tf_op jit(solution)/shard_map/all_gather | solution.py:1054
  136.0 1.6 slice.262
  137.6 0.8 reshape_reshape.3
  138.4 0.8 slice_reduce_fusion
  139.3 0.6 slice_reduce_fusion.2
  139.9 0.6 slice_reduce_fusion.1
  145.1 0.6 slice.233
  145.7 2.4 slice.249
  148.1 0.8 fusion.30
  148.9 0.9 fusion.28
  149.8 0.8 fusion.17
  150.5 0.1 broadcast_in_dim.18
  150.6 0.1 reshape.280
  150.7 2.0 fusion.29
  152.7 0.7 constant_dynamic-update-slice_fusion
  153.4 0.1 slice_dynamic-update-slice_fusion
  153.5 1.0 copy.36.rest_2_
  154.5 0.8 copy.35.rest_1_
  155.2 0.8 copy.38.rest_4_
  156.0 1.0 copy.37.rest_3_
  157.0 0.8 pad_maximum_fusion
  157.8 0.9 copy.34.rest_0_
  158.8 0.6 pad_bitcast_fusion
  159.4 1.7 slice.261.pos_in
  161.1 24.3 %gather_fusion = bf16[4096,256]{1,0:T(8,128)(2,1)} fusion(bf16[34816,256]{1,0:T(8,128)(2,1)} %all-gather.2.cloned.1.call-done, s32[4096]{0:T(1024)S(1)} %copy-done.8), kind=kCustom, calls=%fused_computation | custom fusion | bytes 4210688 | tf_op jit(solution)/shard_map/gather | solution.py:1021
  185.4 3.2 broadcast_in_dim.19.col_ref
  188.6 131.7 %student.1 = (f32[7744,128]{1,0:T(8,128)}, bf16[8,256,512]{2,1,0:T(8,128)(2,1)}, bf16[4096,256]{1,0:T(8,128)(2,1)S(1)}, f32[8,512]{1,0:T(8,128)S(1)}) custom-call(s32[8]{0:T(128)} %copy-done.12, s32[8]{0:T(128)} %iota_multiply_fusion.off_ref, s32[8,512]{1,0:T(8,128)} %get-tuple-element.88.slot_ref, f32[1]{0:T(128)} %bitcast.11.fac_ref, ...), custom_call_target="tpu_custom_call" | custom-call | tf_op jit(solution)/shard_map/student/pallas_call | solution.py:508
  320.4 88.4 %conditional.1 = (f32[8,128]{1,0:T(8,128)}, f32[8,128]{1,0:T(8,128)S(1)}, f32[1,1]{1,0:T(1,128)}, f32[1,1]{1,0:T(1,128)}, f32[1,1]{1,0:T(1,128)}, /*index=5*/f32...) conditional(s32[]{:T(128)} %convert_element_type.42, ...), branch_computations={%region_7.8_spmd, %region_8.11_spmd} | conditional | flops 2109440 | bytes 141492928 | solution.py:1125
  320.4 82.5 %exchange.1 = (f32[976,256]{1,0:T(8,128)S(1)}, f32[224,128]{1,0:T(8,128)S(1)}, f32[8,128]{1,0:T(8,128)}) custom-call(f32[7744,128]{1,0:T(8,128)} %get-tuple-element.55.refs_0_, f32[8,512]{1,0:T(8,128)S(1)} %get-tuple-element.56.refs_1_, bf16[4096,256]{1,0:T(8,128)(2,1)S(1)} %get-tuple-element.57.refs_2_, s32[256,128]{1,0:T(8,128)S(1)} %get-tuple-element.58.refs_3_), custom_call_target="tpu_custom_call" | custom-call | tf_op jit(solution)/shard_map/cond/branch_0_fun/exchange/pallas_call | solution.py:889
  402.9 1.3 fusion.26
  406.8 0.7 copy.80
  407.4 0.7 copy.74
  408.9 1.7 multiply_subtract_fusion.1
  410.6 3.6 multiply_subtract_fusion
  (62 shorter events, 0.5 us)
Async XLA Ops:
  7.2 5.8 %copy-start.13 = (s32[8]{0:T(128)S(1)}, s32[8]{0:T(128)}, u32[]{:S(2)}) copy-start(s32[8]{0:T(128)} %param.15) | copy-start | bytes 100
  7.2 6.4 %copy-start.10 = (s32[8,512]{1,0:T(8,128)S(1)}, s32[8,512]{1,0:T(8,128)}, u32[]{:S(2)}) copy-start(s32[8,512]{1,0:T(8,128)} %param.14) | copy-start | bytes 49156
  7.2 12.9 %copy-start.2 = (bf16[790016]{0:T(1024)(128)(2,1)S(1)}, bf16[790016]{0:T(1024)(128)(2,1)}, u32[]{:S(2)}) copy-start(bf16[790016]{0:T(1024)(128)(2,1)} %param.19) | copy-start | bytes 4740100
  7.2 128.8 %all-gather.2.cloned.1.call-start = ((), (), s32[]{:S(2)}) async-start(), calls=%async_computation.2 | async-start | bytes 18382848 | tf_op jit(solution)/shard_map/all_gather | solution.py:1054
  9.6 11.0 %copy-start.14 = (f32[2]{0:T(128)S(1)}, f32[2]{0:T(128)}, u32[]{:S(2)}) copy-start(f32[2]{0:T(128)} %param.17) | copy-start | bytes 28
  13.6 14.7 %collective-permute-start = (s32[5,512]{1,0:T(8,128)S(1)}, s32[5,512]{1,0:T(8,128)S(1)}, u32[]{:S(2)}, u32[]{:S(2)}) collective-permute-start(s32[5,512]{1,0:T(8,128)S(1)} %pad_add_fusion), channel_id=1, source_target_pairs={{0,31},{1,30},{2,29},{3,28},{4,27},{5,26},{6,25},{7,24},{8,23},{9,... | collective-permute-start | bytes 30728 | tf_op jit(solution)/shard_map/ppermute | solution.py:1060
  29.1 44.2 %copy-start.12 = (s32[8]{0:T(128)}, s32[8]{0:T(128)S(1)}, u32[]{:S(2)}) copy-start(s32[8]{0:T(128)S(1)} %pad_add_fusion.2.len_ref) | copy-start | bytes 100
  46.9 0.7 copy-start.4
  138.4 6.1 %copy-start.1 = (bf16[860160]{0:T(1024)(128)(2,1)}, bf16[860160]{0:T(1024)(128)(2,1)S(1)}, u32[]{:S(2)}) copy-start(bf16[860160]{0:T(1024)(128)(2,1)S(1)} %reshape_reshape.3) | copy-start | bytes 5160964
  148.1 1.6 copy-start.11
  148.1 4.5 %copy-start.9 = (f32[5120]{0:T(1024)S(1)}, f32[5120]{0:T(1024)}, u32[]{:S(2)}) copy-start(f32[5120]{0:T(1024)} %custom-call) | copy-start | bytes 61444
  154.5 6.6 %copy-start.8 = (s32[4096]{0:T(1024)S(1)}, s32[4096]{0:T(1024)}, u32[]{:S(2)}) copy-start(s32[4096]{0:T(1024)} %broadcast_clamp_fusion.1) | copy-start | bytes 49156
  188.6 131.7 %copy-start.5 = (s32[256,128]{1,0:T(8,128)S(1)}, s32[256,128]{1,0:T(8,128)}, u32[]{:S(2)}) copy-start(s32[256,128]{1,0:T(8,128)} %copy-done.4) | copy-start | bytes 393220
  188.6 131.7 %copy-start.7 = (s32[8,512]{1,0:T(8,128)S(1)}, s32[8,512]{1,0:T(8,128)}, u32[]{:S(2)}) copy-start(s32[8,512]{1,0:T(8,128)} %get-tuple-element.154) | copy-start | bytes 49156
  320.3 88.5 %copy-start.3 = (f32[26880]{0:T(1024)S(1)}, f32[26880]{0:T(1024)}, u32[]{:S(2)}) copy-start(f32[26880]{0:T(1024)} %param.23) | copy-start | bytes 322564
  320.3 88.5 %copy-start.6 = (f32[26880]{0:T(1024)S(1)}, f32[26880]{0:T(1024)}, u32[]{:S(2)}) copy-start(f32[26880]{0:T(1024)} %param.24) | copy-start | bytes 322564
  320.4 90.2 %copy-start = (f32[976,256]{1,0:T(8,128)S(1)}, f32[976,256]{1,0:T(8,128)}, u32[]{:S(2)}) copy-start(f32[976,256]{1,0:T(8,128)} %param.20) | copy-start | bytes 2998276
Sparse Core Ops, SparseCore 0:
  13.1 122.8 all-gather.1

commit v3 on v2

--- a/solution.py
+++ b/solution.py
@@ -17,9 +17,20 @@
 NPAR = 856836
 LANES = 128
 norm_eps = 1e-12
+clip_norm = 0.002
+learn_rate = 0.015
+beta_one = 0.9
+beta_two = 0.999
+adam_eps = 1e-08
+decay_rate = 0.01
+sparse_target = 0.3
+ADAM_STEP = 10
+relaxation_heat = 2.0 / 3.0
+widened_left_limit = -0.1
+widened_right_limit = 1.1
 f32 = jnp.float32
 bf16 = jnp.bfloat16
-VMEM_LIMIT = 56 * 2**20
+VMEM_LIMIT = 60 * 2**20
 
 C_GH = 10 * D
 C_HEAD = 11 * D
@@ -89,10 +100,9 @@
     return half_erf
 
 
-def forward_body(span, offset, length, student, rows_ref, pos_ref, col_ref, w, sc, eyes):
+def forward_body(span, length, student, embed, pos_ref, col_ref, w, sc, eyes):
     for c, width in chunks(span):
-        tokens = rows_ref[pl.ds(offset + c, width), :]
-        embedded = nt(eyes[D], tokens) + pos_ref[:, c : c + width]
+        embedded = embed(c, width) + pos_ref[:, c : c + width]
         hat, scale = standardise(embedded)
         start = hat * wide(col_ref, 0, D, width) + wide(col_ref, D, D, width)
         if student:
@@ -169,7 +179,7 @@
         sc["out"][:, c : c + width] = out
 
 
-def backward_body(span, length, factor, target_ref, col_ref, w, sc, acc, add_ref, loss_ref, grad_ref, pos_add, eyes):
+def backward_body(span, length, factor, target_ref, col_ref, w, sc, acc, add_ref, loss_ref, grad_ref, pos_add):
     def add(row, values):
         add_ref[row : row + values.shape[0], :] += lanes_in(values)
 
@@ -259,9 +269,31 @@
         pos_add[:, cols] += d_embedded
         d_low = d_embedded.astype(bf16)
         grad_ref[0, :, cols] = d_low
-        sc["grad_rows"][cols, :] = nt(eyes[width], d_low)
     if span < LEN:
         grad_ref[0, :, span:LEN] = jnp.zeros((D, LEN - span), bf16)
+
+
+def mark_slots(span, slot, perm_ref):
+    step = 512
+
+    def mark(i, carry):
+        rows = pl.ds(pl.multiple_of(i * step, step), step)
+        seen = lax.broadcasted_iota(jnp.int32, (step, span), 0) == slot - i * step
+        perm_ref[rows, 0:span] = seen.astype(f32).astype(bf16)
+        return carry
+
+    lax.fori_loop(0, perm_ref.shape[0] // step, mark, 0)
+
+
+def pack_rows(span, perm_ref, grad_ref, packed_ref):
+    step = 2048
+
+    def add(i, carry):
+        rows = pl.ds(pl.multiple_of(i * step, step), step)
+        packed_ref[rows, :] += nt(perm_ref[rows, 0:span], grad_ref[0, :, 0:span]).astype(bf16)
+        return carry
+
+    lax.fori_loop(0, packed_ref.shape[0] // step, add, 0)
 
 
 SPANS = (256, 384, 512)
@@ -285,15 +317,103 @@
         pos_ref[:, c : c + 256] = nt(eyes_refs[256][...], pos_in[c : c + 256, :])
 
 
-TEACHER_W = (("qkvT", (3 * D, D)), ("oT", (D, D)), ("upT", (FF, D)), ("downT", (D, FF)))
-STUDENT_W = TEACHER_W + (
-    ("aT", (D, D)),
+TEACHER_W = (
     ("qkv", (D, 3 * D)),
+    ("qkvT", (3 * D, D)),
     ("o", (D, D)),
-    ("a", (D, D)),
+    ("oT", (D, D)),
     ("up", (D, FF)),
+    ("upT", (FF, D)),
     ("down", (FF, D)),
+    ("downT", (D, FF)),
 )
+STUDENT_W = TEACHER_W + (("a", (D, D)), ("aT", (D, D)))
+
+
+def spread(col_ref, at, row):
+    col_ref[at : at + LANES, :] = jnp.transpose(jnp.broadcast_to(row, (LANES, LANES)))
+
+
+def load_weights(flat, w, col_ref, one, student):
+    squares = [("qkv", 0), ("qkv", D), ("qkv", 2 * D), ("o", 0)] + ([("a", 0)] if student else [])
+    for i, (name, at) in enumerate(squares):
+        for j in range(2):
+            lanes = slice(at + j * LANES, at + (j + 1) * LANES)
+            w[name][:, lanes] = flat[pl.ds(512 * i + j, D, stride=2), :].astype(bf16)
+    base = 512 * len(squares)
+    for j in range(8):
+        w["up"][:, j * LANES : (j + 1) * LANES] = flat[pl.ds(base + j, D, stride=8), :].astype(bf16)
+    base = base + 2048
+    for j in range(2):
+        w["down"][:, j * LANES : (j + 1) * LANES] = flat[pl.ds(base + j, FF, stride=2), :].astype(
+            bf16
+        )
+    base = base + 2048
+    for i in range(20):
+        spread(col_ref, i * LANES, flat[base + i : base + i + 1, :])
+    for j in range(8):
+        spread(col_ref, C_BUP + j * LANES, flat[base + 20 + j : base + 21 + j, :])
+    unit = one[...]
+    for name in ("qkv", "o", "up") + (("a",) if student else ()):
+        for b in range(0, w[name].shape[1], D):
+            w[name + "T"][b : b + D, :] = nt(unit, w[name][:, b : b + D]).astype(bf16)
+    for b in range(0, FF, D):
+        w["downT"][:, b : b + D] = nt(unit, w["down"][b : b + D, :]).astype(bf16)
+
+
+def total_of(x):
+    return jnp.sum(jnp.sum(x, axis=0, keepdims=True), axis=1, keepdims=True)
+
+
+def head_groups():
+    return (
+        lax.broadcasted_iota(jnp.int32, (D, LANES), 0) // HD
+        == lax.broadcasted_iota(jnp.int32, (D, LANES), 1)
+    ).astype(f32)
+
+
+def load_gates(logits, noise, lagrange_ref, lag_weight, col_ref, slope_ref, lag_ref):
+    index = lax.broadcasted_iota(
+        jnp.int32, logits.shape, 0
+    ) * LANES + lax.broadcasted_iota(jnp.int32, logits.shape, 1)
+    hidden, heads = index < D, (index >= D) & (index < D + HEADS)
+    inner = (index >= D + HEADS) & (index < D + HEADS + FF)
+    logistic = jax.nn.sigmoid((jnp.log(noise) - jnp.log(1.0 - noise) + logits) / relaxation_heat)
+    spanned = widened_right_limit - widened_left_limit
+    stretched = logistic * spanned + widened_left_limit
+    gates = jnp.clip(stretched, 0.0, 1.0)
+    inside = jnp.where((stretched > 0.0) & (stretched < 1.0), 1.0, 0.0)
+    inside = jnp.where((stretched == 0.0) | (stretched == 1.0), 0.5, inside)
+    slope_ref[...] = inside * logistic * (1.0 - logistic) * (spanned / relaxation_heat)
+    keep = jax.nn.sigmoid(
+        logits - relaxation_heat * math.log(-widened_left_limit / widened_right_limit)
+    )
+    kept = total_of(jnp.where(hidden, keep, 0.0)) * (1.0 / D)
+    rest = total_of(jnp.where(heads, keep * (4.0 * HD), 0.0) + jnp.where(inner, keep * 2.0, 0.0))
+    scale = 1.0 / (4.0 * D + 2.0 * FF)
+    excess = kept * rest * scale - sparse_target
+    rate = (lagrange_ref[0] + 2.0 * lagrange_ref[1] * excess) * (scale * lag_weight)
+    share = jnp.where(hidden, rest * (1.0 / D), 0.0)
+    share = share + kept * (jnp.where(heads, 4.0 * HD, 0.0) + jnp.where(inner, 2.0, 0.0))
+    lag_ref[...] = rate * share * (keep * (1.0 - keep))
+    for j in range(2):
+        spread(col_ref, C_GH + j * LANES, gates[j : j + 1, :])
+    wide_heads = lax.dot_general(
+        jnp.broadcast_to(gates[2:3, :], (8, LANES)),
+        head_groups(),
+        (((1,), (1,)), ((), ())),
+        preferred_element_type=f32,
+        precision=lax.Precision.HIGHEST,
+    )
+    for j in range(2):
+        spread(col_ref, C_HEAD + j * LANES, wide_heads[0:1, j * LANES : (j + 1) * LANES])
+    run = jnp.concatenate([gates[j : j + 1, :] for j in range(2, 11)], axis=1)
+    run = pltpu.roll(jnp.broadcast_to(run, (8, 9 * LANES)), 9 * LANES - HEADS, 1)
+    for j in range(8):
+        spread(col_ref, C_GI + j * LANES, run[0:1, j * LANES : (j + 1) * LANES])
+    return lagrange_ref[0] * excess + lagrange_ref[1] * excess * excess
+
+
 TEACHER_S = (
     ("start", (D, LEN), f32),
     ("start_low", (D, LEN), bf16),
@@ -325,7 +445,6 @@
     ("d_context", (D, LEN), bf16),
     ("delta", (8, LEN), f32),
     ("d_qkv", (3 * D, LEN), bf16),
-    ("grad_rows", (LEN, D), f32),
 )
 ACCS = (
     ("qkv", (D, 3 * D)),
@@ -336,76 +455,84 @@
 )
 
 
-def teacher_kernel(len_ref, off_ref, rows_ref, pos_in, col_ref, *rest):
-    w = {name: rest[i] for i, (name, _) in enumerate(TEACHER_W)}
-    out_ref = rest[len(TEACHER_W)]
-    scratch = rest[len(TEACHER_W) + 1 :]
-    sc = {entry[0]: scratch[i] for i, entry in enumerate(TEACHER_S)}
-    pos_ref, eye_one, eye_two = scratch[len(TEACHER_S) :]
+class Eyes:
+    def __init__(self, one, two):
+        self.refs = {128: one, 256: two}
+
+    def __getitem__(self, size):
+        return self.refs[size][...]
+
+
+def student_kernel(n, flat_len, sparse, len_ref, fac_ref, lagrange_ref, noise_ref, flat_in, pos_in, target_ref, *rest):
+    plane, planes, flat_seg = plan(n, flat_len)[:3]
+    cap = room(n)
+    if sparse:
+        slot_ref, rows_ref = rest[:2]
+        rest = rest[2:]
+    else:
+        rows_ref = rest[0]
+        rest = rest[1:]
+    flat_ref, grad_ref, loss_ref = rest[:3]
+    rest = rest[3:]
+    if sparse:
+        packed_ref, rows_all, perm_ref = rest[0], rest[1], rest[2]
+        rest = rest[3:]
+    w = {entry[0]: rest[i] for i, entry in enumerate(STUDENT_W)}
+    rest = rest[len(STUDENT_W) :]
+    sc = {entry[0]: rest[i] for i, entry in enumerate(STUDENT_S)}
+    rest = rest[len(STUDENT_S) :]
+    acc = {entry[0]: rest[i] for i, entry in enumerate(ACCS)}
+    add_ref, pos_add, slope_ref, lag_ref, col_ref, pos_ref, eye_one, eye_two = rest[len(ACCS) :]
     s = pl.program_id(0)
-    sc["out"] = out_ref.at[0]
+    eyes = Eyes(eye_one, eye_two)
 
     @pl.when(s == 0)
     def _():
-        set_up(pos_in, pos_ref, {128: eye_one, 256: eye_two})
-
-    eyes = {128: eye_one, 256: eye_two}
-
-    class Read:
-        def __getitem__(self, size):
-            return eyes[size][...]
+        set_up(pos_in, pos_ref, eyes.refs)
+        for o in range(n):
+            c = o // 2
+            flat_ref[o * flat_seg : (o + 1) * flat_seg, :] = flat_in[
+                o % 2, c % plane, c // plane, :, :
+            ].astype(f32)[:flat_seg]
+        load_weights(flat_ref, w, col_ref, eye_two, True)
+        lag_value = load_gates(
+            flat_ref[R_LOGIT : R_LOGIT + 16, :],
+            noise_ref[...],
+            lagrange_ref,
+            fac_ref[1],
+            col_ref,
+            slope_ref,
+            lag_ref,
+        )
+        for ref in list(acc.values()) + [add_ref, pos_add]:
+            ref[...] = jnp.zeros(ref.shape, f32)
+        row = lax.broadcasted_iota(jnp.int32, (8, LEN), 0)
+        loss_ref[...] = jnp.where(row == 1, lag_value, 0.0)
+        if sparse:
+            packed_ref[...] = jnp.zeros(packed_ref.shape, bf16)
+            for o in range(n):
+                rows_all[:, o * cap : (o + 1) * cap] = rows_ref[o]
 
     length = len_ref[s]
 
     def body(span):
-        offset = pl.multiple_of(off_ref[s], 16)
-        forward_body(span, offset, length, False, rows_ref, pos_ref, col_ref, w, sc, Read())
+        if sparse:
+            mark_slots(span, slot_ref[pl.ds(s, 1), 0:span], perm_ref)
+
+        def embed(c, width):
+            if sparse:
+                return nn(rows_all[...], perm_ref[:, c : c + width])
+            at = pl.multiple_of(s * LEN + c, 128)
+            return nt(eyes[D], rows_ref[pl.ds(at, width), :])
+
+        forward_body(span, length, True, embed, pos_ref, col_ref, w, sc, eyes)
+        backward_body(
+            span, length, fac_ref[0], target_ref, col_ref, w, sc, acc, add_ref, loss_ref, grad_ref, pos_add
+        )
+        if sparse:
+            pack_rows(span, perm_ref, grad_ref, packed_ref)
 
     by_span(length, body)
-
-
-def student_kernel(flat_len, len_ref, off_ref, slot_ref, fac_ref, rows_ref, pos_in, target_ref, col_ref, slope_in, lag_in, *rest):
-    w = {name: rest[i] for i, (name, _) in enumerate(STUDENT_W)}
-    rest = rest[len(STUDENT_W) :]
-    flat_ref, grad_ref, packed_ref, loss_ref = rest[:4]
-    scratch = rest[4:]
-    sc = {entry[0]: scratch[i] for i, entry in enumerate(STUDENT_S)}
-    scratch = scratch[len(STUDENT_S) :]
-    acc = {entry[0]: scratch[i] for i, entry in enumerate(ACCS)}
-    add_ref, pos_add, slots_f32, pos_ref, eye_one, eye_two = scratch[len(ACCS) :]
-    s = pl.program_id(0)
-
-    @pl.when(s == 0)
-    def _():
-        set_up(pos_in, pos_ref, {128: eye_one, 256: eye_two})
-        for ref in list(acc.values()) + [add_ref, pos_add, loss_ref, slots_f32]:
-            ref[...] = jnp.zeros(ref.shape, f32)
-
-    eyes = {128: eye_one, 256: eye_two}
-
-    class Read:
-        def __getitem__(self, size):
-            return eyes[size][...]
-
-    length = len_ref[s]
-
-    def body(span):
-        offset = pl.multiple_of(off_ref[s], 16)
-        forward_body(span, offset, length, True, rows_ref, pos_ref, col_ref, w, sc, Read())
-        backward_body(
-            span, length, fac_ref[0], target_ref, col_ref, w, sc, acc, add_ref, loss_ref, grad_ref, pos_add, Read()
-        )
-
-    by_span(length, body)
-
-    def place(step, carry):
-        for u in range(8):
-            at = step * 8 + u
-            slot = slot_ref[s, at]
-            slots_f32[pl.ds(slot, 1), :] = sc["grad_rows"][pl.ds(at, 1), :]
-        return carry
-
-    lax.fori_loop(0, (length + 7) // 8, place, 0)
 
     @pl.when(s == pl.num_programs(0) - 1)
     def _():
@@ -441,12 +568,11 @@
         for j in range(8):
             flat_ref[R_BUP + j : R_BUP + j + 1, :] = sums[0:1, j * LANES : (j + 1) * LANES]
         hidden = summed(A_GH, D)
-        group = (
-            lax.broadcasted_iota(jnp.int32, (D, LANES), 0) // HD
-            == lax.broadcasted_iota(jnp.int32, (D, LANES), 1)
-        ).astype(f32)
         heads = jnp.dot(
-            summed(A_HEAD, D), group, preferred_element_type=f32, precision=lax.Precision.HIGHEST
+            summed(A_HEAD, D),
+            head_groups(),
+            preferred_element_type=f32,
+            precision=lax.Precision.HIGHEST,
         )
         inner = summed(A_GI, FF)
         moved = pltpu.roll(jnp.concatenate([inner, jnp.zeros((8, LANES), f32)], axis=1), HEADS, 1)
@@ -457,14 +583,13 @@
         ]
         for j, piece in enumerate(tail):
             flat_ref[R_LOGIT + j : R_LOGIT + j + 1, :] = (
-                piece[0:1] * slope_in[j : j + 1, :] + lag_in[j : j + 1, :]
+                piece[0:1] * slope_ref[j : j + 1, :] + lag_ref[j : j + 1, :]
             )
         flat_ref[R_USED:flat_len, :] = jnp.zeros((flat_len - R_USED, LANES), f32)
         for j in range(2):
             flat_ref[pl.ds(flat_len + j, LEN, stride=2), :] = jnp.transpose(
                 pos_add[j * LANES : (j + 1) * LANES, :]
             )
-        packed_ref[...] = slots_f32[0 : packed_ref.shape[0], :].astype(bf16)
 
 
 def whole_spec():
@@ -479,81 +604,59 @@
     return pl.BlockSpec((1, D, LEN), lambda s: (s, 0, 0))
 
 
-def extra_scratch():
+def common_scratch():
     return [
+        pltpu.VMEM((C_ROWS, LANES), f32),
         pltpu.VMEM((D, LEN), f32),
         pltpu.VMEM((128, 128), bf16),
         pltpu.VMEM((256, 256), bf16),
     ]
 
 
-def run_teacher(lengths, offsets, rows, places, columns, weights):
+def run_student(n, flat_len, sparse, lengths, factors, lagrange, noise, flat_all, places, target, given):
     seqs = lengths.shape[0]
+    slot_rows = n * room(n)
+    shapes = [
+        jax.ShapeDtypeStruct((flat_len + 2 * LEN, LANES), f32),
+        jax.ShapeDtypeStruct((seqs, D, LEN), bf16),
+        jax.ShapeDtypeStruct((8, LEN), f32),
+    ]
+    out_specs = [whole_spec(), seq_spec(), whole_spec()]
+    scratch = []
+    if sparse:
+        shapes.append(jax.ShapeDtypeStruct((slot_rows, D), bf16))
+        out_specs.append(whole_spec())
+        scratch = [pltpu.VMEM((D, slot_rows), bf16), pltpu.VMEM((slot_rows, LEN), bf16)]
     return pl.pallas_call(
-        teacher_kernel,
+        functools.partial(student_kernel, n, flat_len, sparse),
         grid=(seqs,),
-        out_shape=jax.ShapeDtypeStruct((seqs, D, LEN), f32),
-        in_specs=[smem_spec(), smem_spec()] + [whole_spec()] * (3 + len(TEACHER_W)),
-        out_specs=seq_spec(),
-        scratch_shapes=[pltpu.VMEM(shape, kind) for _, shape, kind in TEACHER_S] + extra_scratch(),
-        compiler_params=pltpu.CompilerParams(vmem_limit_bytes=VMEM_LIMIT),
-        name="teacher",
-    )(lengths, offsets, rows, places, columns, *[weights[name] for name, _ in TEACHER_W])
-
-
-def run_student(
-    lengths, offsets, slots, factor, rows, places, target, columns, slopes, lag, weights, flat_len, slot_rows
-):
-    seqs = lengths.shape[0]
-    return pl.pallas_call(
-        functools.partial(student_kernel, flat_len),
-        grid=(seqs,),
-        out_shape=(
-            jax.ShapeDtypeStruct((flat_len + 2 * LEN, LANES), f32),
-            jax.ShapeDtypeStruct((seqs, D, LEN), bf16),
-            jax.ShapeDtypeStruct((slot_rows, D), bf16),
-            jax.ShapeDtypeStruct((8, LEN), f32),
-        ),
-        in_specs=[smem_spec()] * 4
-        + [whole_spec()] * 2
+        out_shape=tuple(shapes),
+        in_specs=[smem_spec()] * 3
+        + [whole_spec()] * 3
         + [seq_spec()]
-        + [whole_spec()] * (3 + len(STUDENT_W)),
-        out_specs=(
-            pl.BlockSpec((flat_len + 2 * LEN, LANES), lambda s: (0, 0)),
-            seq_spec(),
-            pl.BlockSpec((slot_rows, D), lambda s: (0, 0)),
-            pl.BlockSpec((8, LEN), lambda s: (0, 0)),
-        ),
-        scratch_shapes=[pltpu.VMEM(shape, kind) for _, shape, kind in STUDENT_S]
+        + [whole_spec()] * len(given),
+        out_specs=tuple(out_specs),
+        scratch_shapes=scratch
+        + [pltpu.VMEM(shape, bf16) for _, shape in STUDENT_W]
+        + [pltpu.VMEM(shape, kind) for _, shape, kind in STUDENT_S]
         + [pltpu.VMEM(shape, f32) for _, shape in ACCS]
         + [
             pltpu.VMEM((A_ROWS, LANES), f32),
             pltpu.VMEM((D, LEN), f32),
-            pltpu.VMEM((slot_rows + 8, D), f32),
+            pltpu.VMEM((16, LANES), f32),
+            pltpu.VMEM((16, LANES), f32),
         ]
-        + extra_scratch(),
+        + common_scratch(),
         compiler_params=pltpu.CompilerParams(vmem_limit_bytes=VMEM_LIMIT),
-        name="student",
-    )(
-        lengths,
-        offsets,
-        slots,
-        factor,
-        rows,
-        places,
-        target,
-        columns,
-        slopes,
-        lag,
-        *[weights[name] for name, _ in STUDENT_W],
-    )
+        name="student" if sparse else "student_dense",
+    )(lengths, factors, lagrange, noise, flat_all, places, target, *given)
 
 
 MESH = pl.DeviceIdType.MESH
 
 
 def room(n):
-    return min(LANES, max(32, 8 * LEN // n))
+    return LANES if 8 * LEN // n >= LANES else 0
 
 
 def greet_all(me, n):
@@ -578,17 +681,15 @@
     )
 
 
-def route_kernel(n, owner_ref, local_ref, stat_ref, slot_ref, got_ref, tile_ref, send_sem, recv_sem):
-    me = lax.axis_index("dp")
+def list_rows(n, owner_ref, local_ref, stat, slot_ref, tile_ref):
     cap = room(n)
-    seqs = owner_ref.shape[0]
     upper = (
         lax.broadcasted_iota(jnp.int32, (256, 256), 0)
         <= lax.broadcasted_iota(jnp.int32, (256, 256), 1)
     ).astype(bf16)
     base = jnp.zeros((n, 1), f32)
     listed = jnp.zeros((n, LANES), f32)
-    for s in range(seqs):
+    for s in range(owner_ref.shape[0]):
         for c in range(0, LEN, 256):
             owner = owner_ref[s : s + 1, c : c + 256]
             mine = (lax.broadcasted_iota(jnp.int32, (n, 256), 0) == owner).astype(f32)
@@ -612,60 +713,300 @@
     tile_ref[...] = jnp.zeros(tile_ref.shape, jnp.int32)
     tile_ref[pl.ds(0, n, stride=8), :] = (listed + 0.5).astype(jnp.int32) - 1
     tile_ref[pl.ds(1, n, stride=8), :] = jnp.where(
-        lane == 0, stat_ref[0], jnp.where(lane == 1, over.astype(jnp.int32), 0)
+        lane == 0, stat, jnp.where(lane == 1, over.astype(jnp.int32), 0)
     )
-    greet_all(me, n)
+
+
+def place_parts(vrows):
+    parts = []
+    for o in range(VOCAB // vrows, (VOCAB + LEN - 1) // vrows + 1):
+        low, top = max(VOCAB, o * vrows), min(VOCAB + LEN, (o + 1) * vrows)
+        parts.append((o, low - o * vrows, low - VOCAB, top - low))
+    return parts
+
+
+def round_up(value, step):
+    return -(-value // step) * step
+
+
+def pair_lists(list_ref, a, cap):
+    return jnp.concatenate(
+        [list_ref[pl.ds(pl.multiple_of(a * 16 + 8 * j, 8), 8), :][0:1, :cap] for j in range(2)],
+        axis=1,
+    )
+
+
+def fetch_kernel(
+    n, flat_len, owner_ref, local_ref, stat_ref, len_ref, rows_ref, pos_in, flat_in, table_ref, own_flat, *rest
+):
+    plane, planes, flat_seg, flat_pad = plan(n, flat_len)[:4]
+    cap = room(n)
+    vrows = table_ref.shape[0]
+    parts = place_parts(vrows)
+    out_ref, got_out, flat_out, place_out = rest[:4]
+    rest = rest[4:]
+    if cap:
+        slot_ref, rows_out = rest[:2]
+        rest = rest[2:]
+    w = {entry[0]: rest[i] for i, entry in enumerate(TEACHER_W)}
+    rest = rest[len(TEACHER_W) :]
+    sc = {entry[0]: rest[i] for i, entry in enumerate(TEACHER_S)}
+    rest = rest[len(TEACHER_S) :]
+    tile_ref, got_ref, flat_all, place_all, pad_ref, flat_f32 = rest[:6]
+    list_sem, a_sem, b_sem, c_sem, pa_sem, pb_sem, pc_sem = rest[6:13]
+    col_ref, pos_ref, eye_one, eye_two = rest[13:17]
+    if cap:
+        table_turned, row_send, rows_in, row_sem = rest[17:]
+    eyes = Eyes(eye_one, eye_two)
+    s = pl.program_id(0)
+    seqs = owner_ref.shape[0]
+    me = lax.axis_index("dp")
+    core = lax.rem(me, 2)
+    chip = me // 2
+    mid = lax.rem(chip, plane)
+    high = chip // plane
+
+    def device(h, m, c):
+        return (h * plane + m) * 2 + c
 
     def tile(ref, i):
         return ref.at[pl.ds(pl.multiple_of(i * 8, 8), 8), :]
 
-    def copy(k):
+    def list_copy(k):
         return copy_to(
-            tile(tile_ref, me ^ k), tile(got_ref, me), send_sem.at[k], recv_sem.at[k], me ^ k
-        )
-
-    def start(k, carry):
-        copy(k).start()
-        return carry
-
-    def finish(k, carry):
-        copy(k).wait()
-        return carry
-
-    lax.fori_loop(1, n, start, 0)
-    own = pl.ds(pl.multiple_of(me * 8, 8), 8)
-    got_ref[own, :] = tile_ref[own, :]
-    lax.fori_loop(1, n, finish, 0)
-
-
-def run_route(n, owner, local, stat):
+            tile(tile_ref, me ^ k), tile(got_ref, me), list_sem.at[0, k], list_sem.at[1, k], me ^ k
+        )
+
+    def row_copy(k):
+        return copy_to(
+            row_send.at[me ^ k], rows_in.at[me], row_sem.at[0, k], row_sem.at[1, k], me ^ k
+        )
+
+    def flat_copies(stage):
+        copies = []
+        if stage == 0:
+            spot = flat_all.at[core, mid, high]
+            for k in range(1, planes):
+                to = device(lax.rem(high + k, planes), mid, core)
+                copies.append(copy_to(spot, spot, a_sem.at[0, k], a_sem.at[1, k], to))
+        elif stage == 1:
+            spot = flat_all.at[core, mid]
+            for k in range(1, plane):
+                to = device(high, lax.rem(mid + k, plane), core)
+                copies.append(copy_to(spot, spot, b_sem.at[0, k], b_sem.at[1, k], to))
+        else:
+            spot = flat_all.at[core]
+            copies.append(copy_to(spot, spot, c_sem.at[0], c_sem.at[1], me ^ 1))
+        return copies
+
+    def place_copies(stage, i):
+        o, _, _, count = parts[i]
+        chip_o = o // 2
+        high_o, mid_o, core_o = chip_o // plane, chip_o % plane, o % 2
+        spot = place_all.at[i, pl.ds(0, round_up(count, 16)), :]
+        same_core, same_mid, same_high = core == core_o, mid == mid_o, high == high_o
+        copies = []
+        if stage == 0:
+            for k in range(1, planes):
+                to = device((high_o + k) % planes, mid_o, core_o)
+                copies.append(copy_to(spot, spot, pa_sem.at[0, i, k], pa_sem.at[1, i, 0], to))
+            sends = same_core & same_mid & same_high
+            receives = same_core & same_mid & (high != high_o)
+        elif stage == 1:
+            for k in range(1, plane):
+                to = device(high, (mid_o + k) % plane, core_o)
+                copies.append(copy_to(spot, spot, pb_sem.at[0, i, k], pb_sem.at[1, i, 0], to))
+            sends = same_core & same_mid
+            receives = same_core & (mid != mid_o)
+        else:
+            copies.append(copy_to(spot, spot, pc_sem.at[0, i], pc_sem.at[1, i], me ^ 1))
+            sends = same_core
+            receives = core != core_o
+        return copies, sends, receives
+
+    def start_stage(stage):
+        for copy in flat_copies(stage):
+            copy.start()
+        for i in range(len(parts)):
+            copies, sends, _ = place_copies(stage, i)
+
+            @pl.when(sends)
+            def _():
+                for copy in copies:
+                    copy.start()
+
+    def finish_stage(stage):
+        for copy in flat_copies(stage):
+            copy.wait()
+        for i in range(len(parts)):
+            copies, sends, receives = place_copies(stage, i)
+
+            @pl.when(sends)
+            def _():
+                for copy in copies:
+                    copy.wait_send()
+
+            @pl.when(receives)
+            def _():
+                copies[0].wait_recv()
+
+    @pl.when(s == 0)
+    def _():
+        greet_all(me, n)
+        pad_ref[...] = jnp.zeros(pad_ref.shape, f32)
+        pad_ref[0:flat_seg, :] = own_flat[...]
+        flat_all[core, mid, high] = pad_ref[...].astype(bf16)
+        for i, (o, at, _, count) in enumerate(parts):
+
+            @pl.when(me == o)
+            def _():
+                full = round_up(count, 16)
+                part = table_ref[at : at + count, :]
+                if full > count:
+                    part = jnp.concatenate([part, jnp.zeros((full - count, D), f32)], axis=0)
+                place_all[i, 0:full, :] = part.astype(bf16)
+
+        start_stage(0)
+        if cap:
+            list_rows(n, owner_ref, local_ref, stat_ref[0], slot_ref, tile_ref)
+        else:
+            tile_ref[...] = jnp.zeros(tile_ref.shape, jnp.int32) + stat_ref[0]
+
+        def start_list(k, carry):
+            list_copy(k).start()
+            return carry
+
+        lax.fori_loop(1, n, start_list, 0)
+        own = pl.ds(pl.multiple_of(me * 8, 8), 8)
+        got_ref[own, :] = tile_ref[own, :]
+        set_up(pos_in, pos_ref, eyes.refs)
+        if cap:
+            table_turned[...] = nt(eye_two[...], table_ref[...].astype(bf16)).astype(bf16)
+
+        def finish_list(k, carry):
+            list_copy(k).wait()
+            return carry
+
+        lax.fori_loop(1, n, finish_list, 0)
+
+        def serve(step, carry):
+            i = n // 2 - 1 - step
+            a = chip ^ i
+            pick = (
+                lax.broadcasted_iota(jnp.int32, (vrows, 2 * cap), 0) == pair_lists(got_ref, a, cap)
+            ).astype(bf16)
+            both = nn(table_turned[...], pick).astype(bf16)
+            for j in range(2):
+                row_send[2 * a + j] = both[:, j * cap : (j + 1) * cap]
+                k = 2 * i + (core ^ j)
+                pl.when(k > 0)(row_copy(k).start)
+            return carry
+
+        if cap:
+            lax.fori_loop(0, n // 2, serve, 0)
+            rows_in[me] = row_send[me]
+        flat_f32[...] = flat_in[...].astype(f32)
+        load_weights(flat_f32, w, col_ref, eye_two, False)
+
+    @pl.when(s == 2)
+    def _():
+        finish_stage(0)
+        start_stage(1)
+
+    @pl.when(s == 4)
+    def _():
+        finish_stage(1)
+        start_stage(2)
+
+    sc["out"] = out_ref.at[0]
+    length = len_ref[s]
+    from_me = jnp.where(s < seqs // 2, me, n - 1 - me)
+    longest = LEN // 3 + (LEN - LEN // 3) * from_me // (n - 1)
+
+    def body(span):
+        def embed(c, width):
+            at = pl.multiple_of(s * LEN + c, 128)
+            return nt(eyes[D], rows_ref[pl.ds(at, width), :])
+
+        forward_body(span, length, False, embed, pos_ref, col_ref, w, sc, eyes)
+
+    by_span(longest, body)
+
+    @pl.when(s == seqs - 1)
+    def _():
+        finish_stage(2)
+
+        def finish_row(k, carry):
+            row_copy(k).wait()
+            return carry
+
+        if cap:
+            lax.fori_loop(1, n, finish_row, 0)
+            rows_out[...] = rows_in[...]
+        got_out[...] = got_ref[...]
+        flat_out[...] = flat_all[...]
+        place_out[...] = place_all[...]
+
+
+def run_fetch(n, flat_len, owner, local, stat, lengths, rows, places, teacher, table, own_flat):
+    plane, planes, flat_seg, flat_pad = plan(n, flat_len)[:4]
+    seqs, cap, vrows = owner.shape[0], room(n), table.shape[0]
+    parts = place_parts(vrows)
+    most = max(round_up(part[3], 16) for part in parts)
+    dma = pltpu.SemaphoreType.DMA
+    got = ((8 * n, LANES), jnp.int32)
+    fetched = ((n, D, cap), bf16)
+    flat_all = ((2, plane, planes, flat_pad, LANES), bf16)
+    place_all = ((len(parts), most, D), bf16)
+    shapes = [((seqs, D, LEN), f32), got, flat_all, place_all]
+    extra = []
+    if cap:
+        shapes += [(owner.shape, jnp.int32), fetched]
+        extra = [
+            pltpu.VMEM((D, vrows), bf16),
+            pltpu.VMEM(*fetched),
+            pltpu.VMEM(*fetched),
+            dma((2, n)),
+        ]
     return pl.pallas_call(
-        functools.partial(route_kernel, n),
-        out_shape=(
-            jax.ShapeDtypeStruct(owner.shape, jnp.int32),
-            jax.ShapeDtypeStruct((8 * n, LANES), jnp.int32),
-        ),
-        in_specs=[whole_spec(), whole_spec(), smem_spec()],
-        out_specs=(whole_spec(), whole_spec()),
-        scratch_shapes=[
-            pltpu.VMEM((8 * n, LANES), jnp.int32),
-            pltpu.SemaphoreType.DMA((n,)),
-            pltpu.SemaphoreType.DMA((n,)),
-        ],
+        functools.partial(fetch_kernel, n, flat_len),
+        grid=(seqs,),
+        out_shape=tuple(jax.ShapeDtypeStruct(shape, kind) for shape, kind in shapes),
+        in_specs=[whole_spec()] * 2 + [smem_spec()] * 2 + [whole_spec()] * 5,
+        out_specs=(seq_spec(),) + (whole_spec(),) * (len(shapes) - 1),
+        scratch_shapes=[pltpu.VMEM(shape, bf16) for _, shape in TEACHER_W]
+        + [pltpu.VMEM(shape, kind) for _, shape, kind in TEACHER_S]
+        + [
+            pltpu.VMEM(*got),
+            pltpu.VMEM(*got),
+            pltpu.VMEM(*flat_all),
+            pltpu.VMEM(*place_all),
+            pltpu.VMEM((flat_pad, LANES), f32),
+            pltpu.VMEM(teacher.shape, f32),
+            dma((2, n)),
+            dma((2, planes)),
+            dma((2, plane)),
+            dma((2,)),
+            dma((2, len(parts), planes)),
+            dma((2, len(parts), plane)),
+            dma((2, len(parts))),
+        ]
+        + common_scratch()
+        + extra,
         compiler_params=pltpu.CompilerParams(
             collective_id=1, has_side_effects=True, vmem_limit_bytes=VMEM_LIMIT
         ),
-        name="route",
-    )(owner, local, stat)
+        name="teacher",
+    )(owner, local, stat, lengths, rows, places, teacher, table, own_flat)
 
 
 def plan(n, flat_len):
     chips = n // 2
     plane = 2 ** ((chips.bit_length() - 1) // 2)
     flat_seg = flat_len // n
-    flat_pad = -(-flat_seg // 16) * 16
+    flat_pad = round_up(flat_seg, 16)
     place_seg = 2 * LEN // n
-    return plane, chips // plane, flat_seg, flat_pad, place_seg, flat_pad + -(-place_seg // 16) * 16
+    return plane, chips // plane, flat_seg, flat_pad, place_seg, flat_pad + round_up(place_seg, 16)
 
 
 def place_tile(n):
@@ -794,13 +1135,7 @@
             pl.when(i > 0)(lambda: row_copy(2 * i).wait_recv())
             row_copy(2 * i + 1).wait_recv()
             a = chip ^ i
-            lists = jnp.concatenate(
-                [
-                    list_ref[pl.ds(pl.multiple_of(a * 16 + 8 * j, 8), 8), :][0:1, :cap]
-                    for j in range(2)
-                ],
-                axis=1,
-            )
+            lists = pair_lists(list_ref, a, cap)
             pick = (lax.broadcasted_iota(jnp.int32, (vrows, 2 * cap), 0) == lists).astype(bf16)
             both = rows_in[pl.ds(pl.multiple_of(a * 2 * cap, 2 * cap), 2 * cap), :]
             table_ref[...] += nn(pick, both)
@@ -814,7 +1149,7 @@
     squares = squares + jnp.sum(
         jnp.sum(grads * grads, axis=0, keepdims=True), axis=1, keepdims=True
     )
-    loss = jnp.sum(jnp.sum(loss_ref[...], axis=0, keepdims=True), axis=1, keepdims=True)
+    loss = jnp.sum(loss_ref[0:1, :], axis=1, keepdims=True)
     lane = lax.broadcasted_iota(jnp.int32, (8, LANES), 1)
     stat_out[...] = jnp.where(lane == 0, squares, jnp.where(lane == 1, loss, 0.0))
 
@@ -915,70 +1250,6 @@
     )(flat_grads, loss_rows, *given)
 
 
-clip_norm = 0.002
-learn_rate = 0.015
-beta_one = 0.9
-beta_two = 0.999
-adam_eps = 1e-08
-decay_rate = 0.01
-sparse_target = 0.3
-ADAM_STEP = 10
-relaxation_heat = 2.0 / 3.0
-widened_left_limit = -0.1
-widened_right_limit = 1.1
-
-
-def layout(student):
-    square = (D, D)
-    entries = [("w_query", square), ("w_key", square), ("w_value", square), ("w_output", square)]
-    if student:
-        entries = entries + [("w_align", square)]
-    entries = entries + [
-        ("w_up", (D, FF)),
-        ("w_down", (FF, D)),
-        ("vectors", (10, D)),
-        ("b_up", (FF,)),
-    ]
-    if student:
-        entries = entries + [("gate_logits", (D + HEADS + FF,))]
-    return entries
-
-
-def unpack(flat_vector, student):
-    pieces = {}
-    offset = 0
-    for entry_name, entry_shape in layout(student):
-        length = math.prod(entry_shape)
-        pieces[entry_name] = flat_vector[offset : offset + length].reshape(entry_shape)
-        offset = offset + length
-    return pieces
-
-
-def gate_values(mask_logodds, flat_random_sample):
-    logistic_function = jax.nn.sigmoid(
-        (jnp.log(flat_random_sample) - jnp.log(1.0 - flat_random_sample) + mask_logodds)
-        / relaxation_heat
-    )
-    return jnp.clip(
-        logistic_function * (widened_right_limit - widened_left_limit) + widened_left_limit,
-        0.0,
-        1.0,
-    )
-
-
-def lagrangian(mask_logodds, lagrange):
-    survival_probability = jax.nn.sigmoid(
-        mask_logodds - relaxation_heat * math.log(-widened_left_limit / widened_right_limit)
-    )
-    kept_hidden = jnp.mean(survival_probability[:D])
-    kept_rest = 4.0 * HD * jnp.sum(survival_probability[D : D + HEADS]) + 2.0 * jnp.sum(
-        survival_probability[D + HEADS :]
-    )
-    expected = kept_hidden * kept_rest / (4.0 * D + 2.0 * FF)
-    excess = expected - sparse_target
-    return lagrange[0] * excess + lagrange[1] * excess * excess
-
-
 def adam_step(weight, first_old, second, clipped):
     first_new = beta_one * first_old + (1.0 - beta_one) * clipped
     second_new = beta_two * second + (1.0 - beta_two) * clipped * clipped
@@ -990,35 +1261,37 @@
     return (weight_new, first_new, second_new)
 
 
-def kernel_weights(pieces, student):
-    w = {}
-    w["qkv"] = jnp.concatenate([pieces["w_query"], pieces["w_key"], pieces["w_value"]], axis=1)
-    w["qkvT"] = w["qkv"].T
-    for name, source in (("o", "w_output"), ("up", "w_up"), ("down", "w_down")):
-        w[name] = pieces[source]
-        w[name + "T"] = pieces[source].T
-    if student:
-        w["a"] = pieces["w_align"]
-        w["aT"] = w["a"].T
-    return w
-
-
-def columns_of(pieces, gates=None):
-    vectors = pieces["vectors"].astype(f32).reshape(-1)
-    bias = pieces["b_up"].astype(f32)
-    if gates is None:
-        gates = jnp.ones((D + HEADS + FF,), f32)
-    parts = [vectors, gates[:D], jnp.repeat(gates[D : D + HEADS], HD), bias, gates[D + HEADS :]]
-    column = jnp.concatenate(parts)
-    return jnp.broadcast_to(column[:, None], (column.shape[0], LANES))
-
-
-def pad_rows(values):
-    return jnp.pad(values, (0, 16 * LANES - values.shape[0])).reshape(16, LANES)
-
-
 def rows_of(table, ids):
     return table.at[ids.reshape(-1)].get(mode="promise_in_bounds")
+
+
+def ring_gather(devices, block):
+    me = lax.axis_index("dp")
+    rows = block.shape[0]
+    onward = [(i, (i + 1) % devices) for i in range(devices)]
+
+    def step(i, state):
+        block, whole = state
+        whole = lax.dynamic_update_slice(whole, block, (lax.rem(me - i + devices, devices) * rows, 0))
+        return lax.ppermute(block, "dp", onward), whole
+
+    whole = jnp.zeros((devices * rows, block.shape[1]), block.dtype)
+    return lax.fori_loop(0, devices, step, (block, whole))[1]
+
+
+def ring_scatter(devices, whole):
+    me = lax.axis_index("dp")
+    rows = whole.shape[0] // devices
+    onward = [(i, (i + 1) % devices) for i in range(devices)]
+
+    def part(i):
+        at = lax.rem(me - 1 - i + 2 * devices, devices) * rows
+        return lax.dynamic_slice(whole, (at, 0), (rows, whole.shape[1]))
+
+    def step(i, total):
+        return lax.ppermute(total, "dp", onward) + part(i)
+
+    return lax.fori_loop(1, devices, step, part(0))
 
 
 def per_device(
@@ -1039,19 +1312,8 @@
     seqs = token_ids.shape[0]
     half = seqs // 2
     vrows = word_table.shape[0]
-    flat_len = layer_flat.shape[0] * devices // LANES
     own = layer_flat.shape[0]
-    own_rows = -(-own // D)
-    pad = -(vrows + own_rows) % 16
-    block = vrows + own_rows + pad
-    shard = jnp.concatenate(
-        [
-            word_table.astype(bf16),
-            jnp.pad(layer_flat.astype(bf16), (0, own_rows * D - own)).reshape(own_rows, D),
-            jnp.zeros((pad, D), bf16),
-        ]
-    )
-    gathered = lax.all_gather(shard, "dp", axis=0, tiled=True)
+    flat_len = own * devices // LANES
 
     mates = [(i, devices - 1 - i) for i in range(devices)]
     sent = jnp.concatenate(
@@ -1060,69 +1322,73 @@
     got = lax.ppermute(sent, "dp", mates)
     ids = jnp.concatenate([token_ids[:half], got[:half]])
     lens = jnp.concatenate([lengths[:half], got[half, :half]])
-    offsets = jnp.arange(seqs, dtype=jnp.int32) * LEN
 
     owner = ids // vrows
     valid = jnp.arange(LEN)[None, :] < lens[:, None]
-    slots, listed = run_route(
+    target, listed, flat_all, place_all, *routed = run_fetch(
         devices,
+        flat_len,
         jnp.where(valid, owner, -1),
         (ids - owner * vrows + 1).astype(f32),
         jnp.sum(lens).reshape(1),
+        lens,
+        rows_of(teacher_table, ids),
+        teacher_table[VOCAB : VOCAB + LEN],
+        teacher_flat.reshape(-1, LANES),
+        word_table,
+        layer_flat.reshape(-1, LANES),
     )
     stats = listed.reshape(devices, 8, LANES)[:, 1, :2]
     global_count = jnp.sum(stats[:, 0]).astype(f32)
-    crowded = jnp.max(stats[:, 1]) > 0
-    factor = ((2.0 / D) / global_count).reshape(1)
-
-    teacher = unpack(teacher_flat, False)
-    target = run_teacher(
+    lag_weight = jnp.where(lax.axis_index("dp") == 0, 1.0, 0.0).astype(f32)
+    factors = jnp.stack([(2.0 / D) / global_count, lag_weight])
+    noise = jnp.pad(gate_noise, (0, 16 * LANES - gate_noise.shape[0]), constant_values=0.5)
+    places = [place_all[i, : part[3]] for i, part in enumerate(place_parts(vrows))]
+    shared = (
         lens,
-        offsets,
-        rows_of(teacher_table, ids),
-        teacher_table[VOCAB : VOCAB + LEN],
-        columns_of(teacher),
-        kernel_weights(teacher, False),
-    )
-
-    blocks = gathered.reshape(devices, block, D)
-    flat_low = blocks[:, vrows : vrows + own_rows].reshape(devices, -1)[:, :own].reshape(-1)
-    pieces = unpack(flat_low, True)
-    logits = pieces["gate_logits"].astype(f32)
-    gates, gate_back = jax.vjp(lambda x: gate_values(x, gate_noise), logits)
-    slopes = gate_back(jnp.ones_like(gates))[0]
-    lag_value, lag_back = jax.vjp(lambda x: lagrangian(x, lagrange), logits)
-    lag_weight = jnp.where(lax.axis_index("dp") == 0, 1.0, 0.0).astype(f32)
-    places = []
-    for o in range(VOCAB // vrows, (VOCAB + LEN - 1) // vrows + 1):
-        low, top = max(VOCAB, o * vrows), min(VOCAB + LEN, (o + 1) * vrows)
-        places.append(gathered[o * (block - vrows) + low : o * (block - vrows) + top])
-    flat_grads, grad_rows, packed, loss_rows = run_student(
-        lens,
-        offsets,
-        slots,
-        factor,
-        rows_of(gathered, ids + owner * (block - vrows)),
+        factors,
+        lagrange,
+        noise.reshape(16, LANES),
+        flat_all,
         jnp.concatenate(places) if len(places) > 1 else places[0],
         target,
-        columns_of(pieces, gates),
-        pad_rows(slopes),
-        pad_rows(lag_back(lag_weight)[0]),
-        kernel_weights(pieces, True),
-        flat_len,
-        devices * room(devices),
     )
 
-    def from_slots(_):
-        return run_exchange(devices, vrows, flat_grads, loss_rows, True, (packed, listed))
-
-    def from_rows(_):
+    def from_slots():
+        slots, fetched = routed
+        flat_grads, _, loss_rows, packed = run_student(
+            devices, flat_len, True, *shared, (slots, fetched)
+        )
+        result = run_exchange(devices, vrows, flat_grads, loss_rows, True, (packed, listed))
+        return (*result, loss_rows)
+
+    def from_rows():
+        if routed:
+            table = ring_gather(devices, word_table.astype(bf16))
+        else:
+            table = lax.all_gather(word_table.astype(bf16), "dp", axis=0, tiled=True)
+        flat_grads, grad_rows, loss_rows = run_student(
+            devices, flat_len, False, *shared, (rows_of(table, ids),)
+        )
         updates = jnp.transpose(grad_rows, (0, 2, 1)).reshape(seqs * LEN, D).astype(f32)
         table = jnp.zeros((devices * vrows, D), f32).at[ids.reshape(-1)].add(updates)
-        table = lax.psum_scatter(table, "dp", scatter_dimension=0, tiled=True)
-        return run_exchange(devices, vrows, flat_grads, loss_rows, False, (table,))
-
-    table_grad, sums, totals = lax.cond(crowded, from_rows, from_slots, 0)
+        if routed:
+            table = ring_scatter(devices, table)
+        else:
+            table = lax.psum_scatter(table, "dp", scatter_dimension=0, tiled=True)
+        result = run_exchange(devices, vrows, flat_grads, loss_rows, False, (table,))
+        return (*result, loss_rows)
+
+    if routed:
+        crowded = jnp.max(stats[:, 1])
+        _, table_grad, sums, totals, loss_rows = lax.while_loop(
+            lambda state: state[0] > 0,
+            lambda state: (jnp.zeros_like(state[0]), *from_rows()),
+            (crowded, *from_slots()),
+        )
+    else:
+        table_grad, sums, totals, loss_rows = from_rows()
+    lag_value = loss_rows[1, 0]
     flat_grad = sums[: own // LANES].reshape(-1)
     grad_norm = jnp.sqrt(totals[0, 0])
     clip = jnp.minimum(1.0, clip_norm / (grad_norm + 1e-06))

time: 431 us -> 390 us (0.905); the launches traced: 423 us -> 387 us
  Pallas kernels: 271 us -> 331 us
  local copies, waits for them, and re-layouts: 83.4 us -> 30.2 us
  between operations: 24.9 us -> 7.35 us
  waiting for transfers between devices: 17.4 us -> 0.01 us
  other arithmetic: 16.6 us -> 9.82 us
    pallas_call x3 -> x2, Pallas kernels: 189 us -> 236 us  [the longest x1 151 us: run_student(): pl.pallas_call(functools.partial(student_kernel, n, flat_len, sparse), gr...]
    gather x2 -> x1, local copies, waits for them, and re-layouts: 47.9 us -> 23.4 us  [rows_of(): return table.at[ids.reshape(-1)].get(mode='promise_in_bounds')]
    all_gather x1 -> x0, waiting for transfers between devices: 17.4 us -> none  [per_device(): gathered = lax.all_gather(shard, 'dp', axis=0, tiled=True)]
    pallas_call x1, Pallas kernels: 82.5 us -> 94.8 us  [run_exchange(): pl.pallas_call(functools.partial(exchange_kernel, n, flat_len, sparse), o...]
    slice x22 -> x1, local copies, waits for them, and re-layouts: 13.1 us -> 1.2 us  [per_device(): lag_value = loss_rows[1, 0]]
    broadcast_in_dim x7 -> x0, local copies, waits for them, and re-layouts: 6.51 us -> none  [the longest x2 6.43 us: columns_of(): return jnp.broadcast_to(column[:, None], (column.shape[0], LANES))]
    transpose x5 -> x0, local copies, waits for them, and re-layouts: 4.48 us -> none  [the longest x3 2.79 us: kernel_weights(): w[name + 'T'] = pieces[source].T]
  transfers between devices with their start and end apart: 2 -> 1, of which waited for: 1 -> 0; matrix products, arithmetic and copies ran while one was open for 9% -> 1% of each run, Pallas kernels for 14% -> 0%
where the time goes in v3:
time: 390 us; the launch traced here: 387 us
  Pallas kernels  331 us (85%)
  local copies, waits for them, and re-layouts  30.2 us (8%)
  other arithmetic  9.82 us (3%)
  between operations  7.35 us (2%)
  starting transfers between devices  6.43 us (2%)
    pallas_call x1, Pallas kernels, run_student(): pl.pallas_call(functools.partial(student_kernel, n, flat_len, sparse), gr...  151 us
    pallas_call x1, Pallas kernels, run_exchange(): pl.pallas_call(functools.partial(exchange_kernel, n, flat_len, sparse), o...  94.8 us
    pallas_call x1, Pallas kernels, run_fetch(): pl.pallas_call(functools.partial(fetch_kernel, n, flat_len), grid=(seqs,)...  85.6 us
    gather x1, local copies, waits for them, and re-layouts, rows_of(): return table.at[ids.reshape(-1)].get(mode='promise_in_bounds')  23.4 us
  transfers between devices with their start and end apart: 1, of which 0 were waited for; matrix products, arithmetic and copies ran while one was open for 1% of the time, Pallas kernels for 0%

profile of v3, /device:TPU:0, one launch (start us, length us, event | category | flops | bytes accessed | tf_op | source)
XLA Modules:
  0.0 387.4 jit_solution(16588611671910435835)
XLA Ops:
  0.6 1.4 slice_reduce_fusion.3
  2.1 0.8 fusion.11
  2.9 6.4 %collective-permute-start.2 = (s32[5,512]{1,0:T(8,128)S(1)}, s32[5,512]{1,0:T(8,128)S(1)}, u32[]{:S(2)}, u32[]{:S(2)}) collective-permute-start(s32[5,512]{1,0:T(8,128)S(1)} %pad_add_fusion), channel_id=1, source_target_pairs={{0,31},{1,30},{2,29},{3,28},{4,27},{5,26},{6,25},{7,24},{8,23},{9,... | collective-permute-start | bytes 30728 | tf_op jit(solution)/shard_map/ppermute | solution.py:1322
  9.3 0.7 pad_bitcast_fusion.noise_ref
  10.0 1.7 slice.48.pos_in
  11.7 1.3 convert.10
  13.0 0.0 collective-permute-done.2
  13.0 0.6 slice_reduce_fusion.2
  13.6 0.1 pad_add_fusion.2.len_ref
  13.7 0.7 pad_add_fusion.1
  14.5 23.4 %gather_fusion.1 = bf16[4096,256]{1,0:T(8,128)(2,1)} fusion(bf16[31034,256]{1,0:T(8,128)(2,1)} %param.22, s32[4096]{0:T(1024)S(1)} %broadcast_clamp_fusion.1), kind=kCustom, calls=%fused_computation.1 | custom fusion | bytes 4210688 | tf_op jit(solution)/shard_map/gather | solution.py:1265
  37.8 0.0 copy-start.6
  39.2 85.6 %teacher.1 = (f32[8,256,512]{2,1,0:T(8,128)}, s32[256,128]{1,0:T(8,128)}, bf16[2,4,4,224,128]{4,3,2,1,0:T(8,128)(2,1)}, bf16[1,512,256]{2,1,0:T(8,128)(2,1)S(1)}...) custom-call(s32[8,512]{1,0:T(8,128)} %get-tuple-element.353.owner_ref, f32[8,512]{1,0:T(8,128)} %get-tuple-element.354.local_ref, ...), custom_call_target="tpu_custom_call" | custom-call | tf_op jit(solution)/shard_map/teacher/pallas_call | solution.py:971
  124.8 0.9 slice.62
  125.7 0.1 copy.23
  125.8 0.6 slice_reduce_fusion
  127.1 0.1 pad_maximum_fusion.fac_ref
  127.2 0.0 copy-done.6
  127.2 150.8 %student.1 = (f32[7744,128]{1,0:T(8,128)}, bf16[8,256,512]{2,1,0:T(8,128)(2,1)}, f32[8,512]{1,0:T(8,128)S(1)}, bf16[4096,256]{1,0:T(8,128)(2,1)}) custom-call(s32[8]{0:T(128)S(1)} %pad_add_fusion.2.len_ref, f32[2]{0:T(128)S(1)} %pad_maximum_fusion.fac_ref, f32[2]{0:T(128)S(1)} %copy-done.6, f32[16,128]{1,0:T(8,128)S(1)} %pad_bitcast_fusion.noise_ref, ...), custom_call_target="tpu_custom_call" | custom-call | tf_op jit(solution)/shard_map/student/pallas_call | solution.py:630
  277.9 0.0 copy-start
  278.0 94.8 %exchange.1 = (f32[976,256]{1,0:T(8,128)}, f32[224,128]{1,0:T(8,128)}, f32[8,128]{1,0:T(8,128)}) custom-call(f32[7744,128]{1,0:T(8,128)} %get-tuple-element.289.refs_0_, f32[8,512]{1,0:T(8,128)S(1)} %get-tuple-element.492.refs_1_, bf16[4096,256]{1,0:T(8,128)(2,1)} %get-tuple-element.291.refs_2_, s32[256,128]{1,0:T(8,128)} %get-tuple-element.283.refs_3_), custom_call_target="tpu_custom_call" | custom-call | tf_op jit(solution)/shard_map/exchange/pallas_call | solution.py:1224
  372.8 0.0 copy-done
  372.8 2.4 while.43
  375.2 0.0 copy-start.2
  375.2 0.0 copy-start.3
  375.2 0.0 copy-start.4
  375.2 0.0 copy-start.5
  375.2 1.3 fusion.12
  378.0 1.2 slice.55
  379.8 4.2 %multiply_subtract_fusion = (f32[976,256]{1,0:T(8,128)}, f32[976,256]{1,0:T(8,128)}, f32[976,256]{1,0:T(8,128)}) fusion(f32[976,256]{1,0:T(8,128)} %table_ref.1, f32[976,256]{1,0:T(8,128)} %get-tuple-element.295, f32[]{:T(128)S(6)} %min.3, f32[976,256]{1,0:T(8,128)} %param.25, f32[976,256]{1,0:T(8,128)} %param.26), kind=kLoop, calls=%fused_computation.12 | loop fusion | flops 3997696 | bytes 6995972 | tf_op jit(solution)/shard_map/sub | solution.py:1258
  384.0 0.0 copy-done.2
  384.0 0.0 copy-done.3
  384.0 0.0 copy-done.4
  384.0 0.0 copy-done.5
  384.1 0.8 multiply_subtract_fusion.1
  (6 shorter events, 0.1 us)
Async XLA Ops:
  2.9 10.1 %collective-permute-start.2 = (s32[5,512]{1,0:T(8,128)S(1)}, s32[5,512]{1,0:T(8,128)S(1)}, u32[]{:S(2)}, u32[]{:S(2)}) collective-permute-start(s32[5,512]{1,0:T(8,128)S(1)} %pad_add_fusion), channel_id=1, source_target_pairs={{0,31},{1,30},{2,29},{3,28},{4,27},{5,26},{6,25},{7,24},{8,23},{9,... | collective-permute-start | bytes 30728 | tf_op jit(solution)/shard_map/ppermute | solution.py:1322
  37.8 89.3 %copy-start.6 = (f32[2]{0:T(128)S(1)}, f32[2]{0:T(128)}, u32[]{:S(2)}) copy-start(f32[2]{0:T(128)} %lagrange_ref.1) | copy-start | bytes 28
  277.9 94.8 %copy-start = (f32[8,512]{1,0:T(8,128)}, f32[8,512]{1,0:T(8,128)S(1)}, u32[]{:S(2)}) copy-start(f32[8,512]{1,0:T(8,128)S(1)} %get-tuple-element.492.refs_1_) | copy-start | bytes 49156
  375.2 8.8 %copy-start.2 = (f32[26880]{0:T(1024)S(1)}, f32[26880]{0:T(1024)}, u32[]{:S(2)}) copy-start(f32[26880]{0:T(1024)} %param.27) | copy-start | bytes 322564
  375.2 8.8 %copy-start.3 = (f32[26880]{0:T(1024)S(1)}, f32[26880]{0:T(1024)}, u32[]{:S(2)}) copy-start(f32[26880]{0:T(1024)} %param.28) | copy-start | bytes 322564
  375.2 8.8 %copy-start.4 = (f32[26880]{0:T(1024)S(1)}, f32[26880]{0:T(1024)}, u32[]{:S(2)}) copy-start(f32[26880]{0:T(1024)} %param.29) | copy-start | bytes 322564
  375.2 8.8 %copy-start.5 = (f32[224,128]{1,0:T(8,128)S(1)}, f32[224,128]{1,0:T(8,128)}, u32[]{:S(2)}) copy-start(f32[224,128]{1,0:T(8,128)} %get-tuple-element.297) | copy-start | bytes 344068
